TPU v7x, 128 devices: a whole 4x4x4 slice. The times are simulated.
128 devices in a mesh: dev: 128 (over y, z, x, core).
Axes of the slice: x: 4, y: 4, z: 4, core: 2. Of those that a mesh axis runs over, the one named last changes fastest.
Arguments:
- upstream: bfloat16 [65536, 1024], P('dev'), may hold values from -24 to 24
- bag: int32 [65536, 8], P('dev'), may hold values from 0 to 767
- next_bag: int32 [65536, 8], P('dev'), may hold values from 0 to 511
- hot_slots: int32 [65536], P('dev'), may hold values from 0 to 8191, as said below
- evict_dest: int32 [128, 128, 2], P('dev'), may hold values from -1 to 1023, as said below
- hot_cache: float32 [65536, 128], P('dev'), may hold values from -6 to 6
- evict_cache: float32 [32768, 128], P('dev'), may hold values from -6 to 6
- hot_table: float32 [8192, 128], P('dev'), may hold values from -6 to 6
- hot_accum: float32 [8192, 128], P('dev'), may hold values from 1 to 100
- owner_table: float32 [131072, 128], P('dev'), may hold values from -6 to 6
- owner_accum: float32 [131072, 128], P('dev'), may hold values from 1 to 30
- cross_w: float32 [2, 1024, 1024], P(None, None, 'dev'), may hold values from -0.1875 to 0.1875
- cross_b: float32 [2, 1024], P(None, 'dev'), may hold values from -3 to 3
- cross_accum: float32 [2, 1024, 1024], P(None, None, 'dev'), may hold values from 10000 to 1000000
Outputs:
- next_first: bfloat16 [65536, 1024], P('dev')
- hot_new: float32 [8192, 128], P('dev')
- hot_accum_new: float32 [8192, 128], P('dev')
- owner_new: float32 [131072, 128], P('dev')
- owner_accum_new: float32 [131072, 128], P('dev')
- cross_w_new: float32 [2, 1024, 1024], P(None, None, 'dev')
- cross_b_new: float32 [2, 1024], P(None, 'dev')
Inputs may be any that keep to these rules, and one draw needn't show every extreme that they name: `hot_slots`: entry d * 512 + 4 * o + k names a row of owner o's block, o * 64 to o * 64 + 63; the 4 rows of one device in one owner's block are distinct. evict_dest[o, s, k] is the row of owner o's block (0 to 1023) that receives the gradient of source s's evicted slot 2 * o + k, or -1 for an empty slot; in each (o, s) bucket the live entries come first, and some bucket is full in every draw.
All inputs are finite; a program needn't handle non-finite values.
Results may differ from a plain program's by a relative error of at most 0.0033.
The roundings to bfloat16 on the way count: a program that leaves them out, or rounds other values in their place, can miss the bound.
Values may be sent and summed in bfloat16 or wider, within the bound.
A program may use at most 128 MiB of HBM per device.

v0:
```python
import jax
import jax.numpy as jnp
from jax import lax
from jax.sharding import PartitionSpec as P

row_rate = 0.05
weight_rate = 0.005
bias_rate = 0.0002
epsilon = 1e-10


def rows_first(arrays, axis, dims):
    turned = [jnp.moveaxis(a, dim, 0) for a, dim in zip(arrays, dims)]
    both = jnp.concatenate([t.reshape(len(t), -1) for t in turned], axis=1)
    filled, at, gathered = (lax.all_gather(both, axis, axis=0, tiled=True), 0, [])
    for t, dim in zip(turned, dims):
        piece = filled[:, at : at + t[0].size].reshape(-1, *t.shape[1:])
        gathered.append(jnp.moveaxis(piece, 0, dim))
        at += t[0].size
    return tuple(gathered)


def adagrad(params, accumulator, gradient, step_rate):
    updated = accumulator + gradient * gradient
    return (params - step_rate * gradient / (jnp.sqrt(updated) + epsilon), updated)


def owner_update(moved, evict_dest, owner_table, owner_accum, width):
    destination = evict_dest[0]
    targets = jnp.where(destination >= 0, destination, owner_table.shape[0]).reshape(-1)
    owner_grad = (
        jnp.zeros(owner_table.shape, jnp.float32)
        .at[targets]
        .add(moved.reshape(-1, width), mode="drop")
    )
    return adagrad(owner_table, owner_accum, owner_grad, row_rate)


def shared_update(arrived_ids, arrived, my_index, hot_table, hot_accum, devices, width):
    block_rows = hot_table.shape[0]
    local_rows = (arrived_ids - my_index * block_rows).reshape(-1)
    block_grad = (
        jnp.zeros(hot_table.shape, jnp.float32).at[local_rows].add(arrived.reshape(-1, width))
    )
    hot_new, hot_accum_new = adagrad(hot_table, hot_accum, block_grad, row_rate)
    returned = jnp.take(hot_new, local_rows, axis=0).reshape(devices, -1, width)
    return (hot_new, hot_accum_new, returned)


def local(
    upstream,
    bag,
    next_bag,
    hot_slots,
    evict_dest,
    hot_cache,
    evict_cache,
    hot_table,
    hot_accum,
    owner_table,
    owner_accum,
    cross_w,
    cross_b,
    cross_accum,
):
    devices = lax.axis_size("dev")
    my_index = lax.axis_index("dev")
    width = hot_cache.shape[1]
    samples = bag.shape[0]
    hot_count = hot_cache.shape[0]
    weights, biases = rows_first(
        (cross_w.astype(jnp.bfloat16), cross_b.astype(jnp.bfloat16)), "dev", (2, 1)
    )
    biases = biases.astype(jnp.float32)
    slot_values = jnp.concatenate([hot_cache, evict_cache], axis=0)
    slot_total = slot_values.shape[0]
    features = jnp.take(slot_values, bag.reshape(-1), axis=0).reshape(samples, -1)
    feat_bf = features.astype(jnp.bfloat16)
    proj_one = jnp.dot(feat_bf, weights[0], preferred_element_type=jnp.float32) + biases[0]
    layer_one = features * proj_one + features
    layer_bf = layer_one.astype(jnp.bfloat16)
    proj_two = jnp.dot(layer_bf, weights[1], preferred_element_type=jnp.float32) + biases[1]
    grad_out = upstream.astype(jnp.float32)
    grad_two = grad_out * features
    grad_two_bf = grad_two.astype(jnp.bfloat16)
    weight_two = jnp.dot(layer_bf.T, grad_two_bf, preferred_element_type=jnp.float32)
    bias_two = jnp.sum(grad_two, axis=0)
    grad_layer = grad_out + jnp.dot(grad_two_bf, weights[1].T, preferred_element_type=jnp.float32)
    grad_one = grad_layer * features
    grad_one_bf = grad_one.astype(jnp.bfloat16)
    weight_one = jnp.dot(feat_bf.T, grad_one_bf, preferred_element_type=jnp.float32)
    bias_one = jnp.sum(grad_one, axis=0)
    weight_shard, bias_shard = (
        lax.psum_scatter(
            jnp.stack([weight_one, weight_two]), "dev", scatter_dimension=2, tiled=True
        ),
        lax.psum_scatter(jnp.stack([bias_one, bias_two]), "dev", scatter_dimension=1, tiled=True),
    )
    grad_feat = grad_out * proj_two + grad_layer * (proj_one + 1.0)
    grad_feat = grad_feat + jnp.dot(grad_one_bf, weights[0].T, preferred_element_type=jnp.float32)
    grad_rows = grad_feat.astype(jnp.bfloat16).reshape(-1, width)
    one_hot = (
        bag.reshape(-1)[:, None]
        == lax.broadcasted_iota(jnp.int32, (grad_rows.shape[0], slot_total), 1)
    ).astype(jnp.bfloat16)
    slot_grad = lax.dot_general(
        one_hot, grad_rows, (((0,), (0,)), ((), ())), preferred_element_type=jnp.float32
    )
    hot_grads = slot_grad[:hot_count].reshape(devices, -1, width)
    evict_grads = slot_grad[hot_count:].reshape(devices, -1, width)
    shared_per = hot_grads.shape[1]
    arrived_ids = lax.all_to_all(
        hot_slots.reshape(devices, -1), "dev", split_axis=0, concat_axis=0, tiled=True
    )
    packed = jnp.concatenate([hot_grads, evict_grads], axis=1)
    unpacked = lax.all_to_all(packed, "dev", split_axis=0, concat_axis=0, tiled=True)
    arrived = unpacked[:, :shared_per]
    moved = unpacked[:, shared_per:]
    hot_new, hot_accum_new, returned = shared_update(
        arrived_ids, arrived, my_index, hot_table, hot_accum, devices, width
    )
    held_rows = lax.all_to_all(returned, "dev", split_axis=0, concat_axis=0, tiled=True).reshape(
        hot_count, width
    )
    owner_new, owner_accum_new = owner_update(moved, evict_dest, owner_table, owner_accum, width)
    cross_w_new, unused = adagrad(cross_w, cross_accum, weight_shard, weight_rate)
    cross_b_new = cross_b - bias_rate * bias_shard
    first_weight, first_bias = rows_first(
        (cross_w_new[0].astype(jnp.bfloat16), cross_b_new[0].astype(jnp.bfloat16)), "dev", (1, 0)
    )
    next_feat = jnp.take(held_rows, next_bag.reshape(-1), axis=0).reshape(next_bag.shape[0], -1)
    proj = jnp.dot(
        next_feat.astype(jnp.bfloat16), first_weight, preferred_element_type=jnp.float32
    ) + first_bias.astype(jnp.float32)
    next_first = (next_feat * proj + next_feat).astype(jnp.bfloat16)
    return (
        next_first,
        hot_new,
        hot_accum_new,
        owner_new,
        owner_accum_new,
        cross_w_new,
        cross_b_new,
    )


def solution(mesh):
    return jax.shard_map(
        local,
        mesh=mesh,
        in_specs=(
            P("dev", None),
            P("dev", None),
            P("dev", None),
            P("dev"),
            P("dev", None, None),
            P("dev", None),
            P("dev", None),
            P("dev", None),
            P("dev", None),
            P("dev", None),
            P("dev", None),
            P(None, None, "dev"),
            P(None, "dev"),
            P(None, None, "dev"),
        ),
        out_specs=(
            P("dev", None),
            P("dev", None),
            P("dev", None),
            P("dev", None),
            P("dev", None),
            P(None, None, "dev"),
            P(None, "dev"),
        ),
        check_vma=False,
    )
```

profile of v0, /device:TPU:1, one launch (start us, length us, event | category | flops | bytes accessed | tf_op | source)
XLA Modules:
  0.0 369.3 jit_solution(14683335172058845515)
XLA Ops:
  11.7 14.1 %gather_fusion = f32[4096,128]{1,0:T(8,128)} fusion(f32[768,128]{1,0:T(8,128)S(1)} %pad_maximum_fusion.2, s32[4096]{0:T(1024)S(1)} %broadcast_clamp_fusion.1), kind=kCustom, calls=%fused_computation | custom fusion | bytes 4210688 | tf_op jit(solution)/shard_map/jit(_take)/gather | solution.py:77
  25.7 1.7 gather.21
  27.7 2.7 fusion.9
  30.4 51.9 %all-gather.3.cloned.1.call-done = bf16[1024,2050]{1,0:T(8,128)(2,1)} async-done(((bf16[8,2050]{1,0:T(8,128)(2,1)}), bf16[1024,2050]{1,0:T(8,128)(2,1)}) %all-gather.3.cloned.1.call-update) | async-done | bytes 4198416 | tf_op jit(solution)/shard_map/all_gather | solution.py:15
  82.3 4.8 %slice.66 = bf16[1024,2048]{1,0:T(8,128)(2,1)} slice(bf16[1024,2050]{1,0:T(8,128)(2,1)} %all-gather.3.cloned.1.call-done), slice={[0:1024], [0:2048]} | slice | bytes 8388608 | tf_op jit(solution)/shard_map/slice | solution.py:17
  87.1 6.4 %copy.92 = bf16[1024,2048]{0,1:T(8,128)(2,1)} copy(bf16[1024,2048]{1,0:T(8,128)(2,1)} %slice.66) | data formatting | bytes 8388608 | tf_op jit(solution)/shard_map/reshape | solution.py:17
  95.0 3.3 fusion.11
  98.3 1.6 broadcast_in_dim.51
  100.0 1.7 multiply_reduce_fusion
  101.6 1.4 convolution_bitcast_fusion.1
  103.0 1.7 convolution_bitcast_fusion
  104.7 4.1 %pad_maximum_fusion = f32[2,1024,1024]{2,1,0:T(8,128)} fusion(f32[1,1024,1024]{2,1,0:T(8,128)S(1)} %convolution_bitcast_fusion, f32[1,1024,1024]{2,1,0:T(8,128)S(1)} %convolution_bitcast_fusion.1), kind=kLoop, calls=%fused_computation.7 | loop fusion | flops 2097152 | bytes 16777216 | tf_op jit(solution)/shard_map/stack | solution.py:95
  108.8 13.4 %copy.86 = f32[2,1024,1024]{1,0,2:T(2,128)} copy(f32[2,1024,1024]{2,1,0:T(8,128)} %pad_maximum_fusion) | data formatting | bytes 16777216 | tf_op jit(solution)/shard_map/stack | solution.py:95
  123.6 5.4 %all-to-all-start = ((s32[128,1,4]{2,1,0:T(1,128)}), s32[128,1,4]{2,1,0:T(1,128)S(1)}, u32[]{:S(2)}, u32[]{:S(2)}) async-start(s32[128,1,4]{2,1,0:T(1,128)} %bitcast), calls=%async_computation | async-start | bytes 131072 | tf_op jit(solution)/shard_map/all_to_all | solution.py:112
  129.4 68.7 %all-reduce.1 = f32[2,1024]{1,0:T(2,128)S(1)} all-reduce(f32[2,1024]{1,0:T(2,128)S(1)} %pad_maximum_fusion.5), channel_id=3, replica_groups=mesh['dev'=128] {'dev'}, use_global_device_ids=true, to_apply=%region_4.5.clone | all-reduce | flops 2048 | bytes 16384
  198.8 82.2 %all-reduce.4.cloned.1.call-done = f32[2,1024,1024]{1,0,2:T(2,128)} async-done(((f32[2,1024,1024]{1,0,2:T(2,128)}), f32[2,1024,1024]{1,0,2:T(2,128)}) %all-reduce.4.cloned.1.call-update) | async-done | bytes 8388624
  284.8 3.7 fusion.10
  289.1 4.9 %fusion.4 = bf16[512,1024]{1,0:T(8,128)(2,1)} fusion(f32[512,1024]{1,0:T(8,128)S(1)} %fusion.10, bf16[512,1024]{1,0:T(8,128)(2,1)S(1)} %copy-done.18, f32[512,1024]{1,0:T(8,128)S(1)} %copy-done.4, f32[512,1024]{1,0:T(8,128)} %copy-done.19, bf16[2,1024,1024]{2,1,0:T(8,128)(2,1)S(1)} %bitcast.104, f32[1024]{0:T(1024)S(1)} %get-tuple-element.38, ...), kind=kOutput, calls=%fused_computation.18 | convolution fusion | flops 1081081856 | bytes 15216640 | tf_op jit(solution)/shard_map/dot_general | solution.py:82
  294.0 1.5 reshape.231
  295.6 4.0 %fusion = f32[768,128]{1,0:T(8,128)S(1)} fusion(bf16[4096,128]{1,0:T(8,128)(2,1)S(1)} %reshape.231, s32[4096]{0:T(1024)S(1)} %eq.10), kind=kOutput, calls=%fused_computation.6 | convolution fusion | flops 808452096 | bytes 1458176 | tf_op jit(solution)/shard_map/dot_general | solution.py:106
  300.6 6.6 %all-to-all-start.1 = ((f32[128,6,128]{2,1,0:T(8,128)}), f32[128,6,128]{2,1,0:T(8,128)S(1)}, u32[]{:S(2)}, u32[]{:S(2)}) async-start(f32[128,6,128]{2,1,0:T(8,128)} %pad_maximum_fusion.1), calls=%async_computation.1 | async-start | bytes 1048576 | tf_op jit(solution)/shard_map/all_to_all | solution.py:116
  307.3 13.7 %all-to-all-done.1 = f32[128,6,128]{2,1,0:T(8,128)S(1)} async-done(((f32[128,6,128]{2,1,0:T(8,128)}), f32[128,6,128]{2,1,0:T(8,128)S(1)}, u32[]{:S(2)}, u32[]{:S(2)}) %all-to-all-start.1) | async-done | bytes 393248 | tf_op jit(solution)/shard_map/all_to_all | solution.py:116
  321.0 2.3 scatter_custom_fusion
  325.9 4.6 %all-to-all-start.2 = ((f32[128,4,128]{2,1,0:T(4,128)}), f32[128,4,128]{2,1,0:T(4,128)S(1)}, u32[]{:S(2)}, u32[]{:S(2)}) async-start(f32[128,4,128]{2,1,0:T(4,128)} %broadcast_select_fusion), calls=%async_computation.2 | async-start | bytes 524288 | tf_op jit(solution)/shard_map/all_to_all | solution.py:122
  330.5 1.6 scatter_custom_fusion.1
  332.1 1.2 divide_subtract_fusion
  333.3 9.2 %all-to-all-done.2 = f32[128,4,128]{2,1,0:T(4,128)S(1)} async-done(((f32[128,4,128]{2,1,0:T(4,128)}), f32[128,4,128]{2,1,0:T(4,128)S(1)}, u32[]{:S(2)}, u32[]{:S(2)}) %all-to-all-start.2) | async-done | bytes 262176 | tf_op jit(solution)/shard_map/all_to_all | solution.py:122
  342.5 10.8 %gather_fusion.2 = f32[4096,128]{1,0:T(8,128)S(1)} fusion(f32[512,128]{1,0:T(8,128)S(1)} %bitcast.95, s32[4096]{0:T(1024)S(1)} %broadcast_clamp_fusion), kind=kCustom, calls=%fused_computation.2 | custom fusion | bytes 4210688 | tf_op jit(solution)/shard_map/jit(_take)/gather | solution.py:131
  353.3 1.5 gather.26
  354.7 1.1 convert_reduce_fusion
  355.8 1.6 broadcast_in_dim.47
  357.5 5.3 %fusion.6 = bf16[512,1024]{1,0:T(8,128)(2,1)} fusion(f32[512,1024]{1,0:T(8,128)} %gather.26, pred[64,8,8,128]{3,2,1,0:T(8,128)(4,1)S(1)} %bitcast.109, bf16[1024,1025]{1,0:T(8,128)(2,1)} %all-gather.5.cloned.1.call-done, f32[1024]{0:T(1024)S(1)} %convert_reduce_fusion), kind=kOutput, calls=%fused_computation.20 | convolution fusion | flops 1077411840 | bytes 8392704 | tf_op jit(solution)/shard_map/dot_general | solution.py:132
  (94 shorter events, 16.5 us)
Async XLA Ops:
  7.2 75.1 %all-gather.3.cloned.1.call-start = ((), (), s32[]{:S(2)}) async-start(), calls=%async_computation.3 | async-start | bytes 4491264 | tf_op jit(solution)/shard_map/all_gather | solution.py:15
  9.5 271.6 %all-reduce.4.cloned.1.call-start = ((), (), s32[]{:S(2)}) async-start(), calls=%async_computation.5 | async-start | bytes 16777216
  25.7 1.7 copy-start.9
  95.0 5.0 %copy-start.1 = (bf16[1024,2048]{0,1:T(8,128)(2,1)S(1)}, bf16[1024,2048]{0,1:T(8,128)(2,1)}, u32[]{:S(2)}) copy-start(bf16[1024,2048]{0,1:T(8,128)(2,1)} %copy.92) | copy-start | bytes 12582916
  95.0 5.0 %copy-start.17 = (bf16[512,1024]{1,0:T(8,128)(2,1)S(1)}, bf16[512,1024]{1,0:T(8,128)(2,1)}, u32[]{:S(2)}) copy-start(bf16[512,1024]{1,0:T(8,128)(2,1)} %param.14) | copy-start | bytes 3145732
  98.3 4.7 %copy-start.19 = (f32[512,1024]{1,0:T(8,128)}, f32[512,1024]{1,0:T(8,128)S(1)}, u32[]{:S(2)}) copy-start(f32[512,1024]{1,0:T(8,128)S(1)} %fusion.11) | copy-start | bytes 6291460
  101.6 1.4 copy-start.3
  122.2 0.7 copy-start.14
  122.2 6.9 %copy-start.10 = (s32[512,8]{0,1:T(8,128)S(1)}, s32[512,8]{0,1:T(8,128)}, u32[]{:S(2)}) copy-start(s32[512,8]{0,1:T(8,128)} %param.16) | copy-start | bytes 49156
  122.2 75.9 %copy-start.16 = (f32[2,8]{1,0:T(2,128)S(1)}, f32[2,8]{1,0:T(2,128)}, u32[]{:S(2)}) copy-start(f32[2,8]{1,0:T(2,128)} %param.26) | copy-start | bytes 196
  122.2 159.7 %copy-start.7 = (f32[2,1024,8]{1,2,0:T(8,128)S(1)}, f32[2,1024,8]{1,2,0:T(8,128)}, u32[]{:S(2)}) copy-start(f32[2,1024,8]{1,2,0:T(8,128)} %param.25) | copy-start | bytes 196612
  122.2 159.7 %copy-start.11 = (f32[2,1024,8]{1,2,0:T(8,128)S(1)}, f32[2,1024,8]{1,2,0:T(8,128)}, u32[]{:S(2)}) copy-start(f32[2,1024,8]{1,2,0:T(8,128)} %param.27) | copy-start | bytes 196612
  122.2 160.4 %copy-start.15 = (s32[1,128,2]{1,2,0:T(2,128)S(1)}, s32[1,128,2]{1,2,0:T(2,128)}, u32[]{:S(2)}) copy-start(s32[1,128,2]{1,2,0:T(2,128)} %param.18) | copy-start | bytes 3076
  123.6 159.7 %all-to-all-start = ((s32[128,1,4]{2,1,0:T(1,128)}), s32[128,1,4]{2,1,0:T(1,128)S(1)}, u32[]{:S(2)}, u32[]{:S(2)}) async-start(s32[128,1,4]{2,1,0:T(1,128)} %bitcast), calls=%async_computation | async-start | bytes 131072 | tf_op jit(solution)/shard_map/all_to_all | solution.py:112
  129.0 225.7 %all-gather.5.cloned.1.call-start = ((), (), s32[]{:S(2)}) async-start(), calls=%async_computation.4 | async-start | bytes 2377728 | tf_op jit(solution)/shard_map/all_gather | solution.py:15
  282.0 6.5 %copy-start.8 = (f32[2,1024,8]{1,2,0:T(8,128)}, f32[2,1024,8]{1,2,0:T(8,128)S(1)}, u32[]{:S(2)}) copy-start(f32[2,1024,8]{1,2,0:T(8,128)S(1)} %divide_subtract_fusion.1) | copy-start | bytes 196612
  284.7 3.7 %copy-start.2 = (bf16[1024,2048]{0,1:T(8,128)(2,1)S(1)}, bf16[1024,2048]{0,1:T(8,128)(2,1)}, u32[]{:S(2)}) copy-start(bf16[1024,2048]{0,1:T(8,128)(2,1)} %copy.92) | copy-start | bytes 12582916
  284.8 4.1 %copy-start.4 = (f32[512,1024]{1,0:T(8,128)S(1)}, f32[512,1024]{1,0:T(8,128)}, u32[]{:S(2)}) copy-start(f32[512,1024]{1,0:T(8,128)} %copy-done.3) | copy-start | bytes 6291460
  284.8 4.3 %copy-start.18 = (bf16[512,1024]{1,0:T(8,128)(2,1)S(1)}, bf16[512,1024]{1,0:T(8,128)(2,1)}, u32[]{:S(2)}) copy-start(bf16[512,1024]{1,0:T(8,128)(2,1)} %param.14) | copy-start | bytes 3145732
  299.6 23.7 %copy-start.12 = (f32[64,128]{1,0:T(8,128)S(1)}, f32[64,128]{1,0:T(8,128)}, u32[]{:S(2)}) copy-start(f32[64,128]{1,0:T(8,128)} %param.21) | copy-start | bytes 98308
  299.6 23.6 %copy-start.13 = (f32[64,128]{1,0:T(8,128)S(1)}, f32[64,128]{1,0:T(8,128)}, u32[]{:S(2)}) copy-start(f32[64,128]{1,0:T(8,128)} %param.22) | copy-start | bytes 98308
  300.6 20.4 %all-to-all-start.1 = ((f32[128,6,128]{2,1,0:T(8,128)}), f32[128,6,128]{2,1,0:T(8,128)S(1)}, u32[]{:S(2)}, u32[]{:S(2)}) async-start(f32[128,6,128]{2,1,0:T(8,128)} %pad_maximum_fusion.1), calls=%async_computation.1 | async-start | bytes 1048576 | tf_op jit(solution)/shard_map/all_to_all | solution.py:116
  323.9 8.2 %copy-start = (f32[64,128]{1,0:T(8,128)}, f32[64,128]{1,0:T(8,128)S(1)}, u32[]{:S(2)}) copy-start(f32[64,128]{1,0:T(8,128)S(1)} %get-tuple-element.43) | copy-start | bytes 98308
  323.9 8.2 %copy-start.5 = (f32[1024,128]{1,0:T(8,128)S(1)}, f32[1024,128]{1,0:T(8,128)}, u32[]{:S(2)}) copy-start(f32[1024,128]{1,0:T(8,128)} %param.23) | copy-start | bytes 1572868
  323.9 8.2 %copy-start.6 = (f32[1024,128]{1,0:T(8,128)S(1)}, f32[1024,128]{1,0:T(8,128)}, u32[]{:S(2)}) copy-start(f32[1024,128]{1,0:T(8,128)} %param.24) | copy-start | bytes 1572868
  325.9 16.6 %all-to-all-start.2 = ((f32[128,4,128]{2,1,0:T(4,128)}), f32[128,4,128]{2,1,0:T(4,128)S(1)}, u32[]{:S(2)}, u32[]{:S(2)}) async-start(f32[128,4,128]{2,1,0:T(4,128)} %broadcast_select_fusion), calls=%async_computation.2 | async-start | bytes 524288 | tf_op jit(solution)/shard_map/all_to_all | solution.py:122
Sparse Core Ops, SparseCore 0:
  11.7 70.5 all-gather.2
  122.4 158.6 all-reduce.3
  284.4 65.2 all-gather.4
where the time goes:
time: 370 us; the launch traced here: 369 us
  waiting for transfers between devices  157 us (42%)
  blocking collectives  68.7 us (19%)
  local copies, waits for them, and re-layouts  64.8 us (18%)
  matrix products  26 us (7%)
  other arithmetic  21.8 us (6%)
  starting transfers between devices  16.7 us (5%)
  between operations  14.3 us (4%)
    unnamed x4, waiting for transfers between devices  82.3 us
    unnamed x1, blocking collectives  68.7 us
    all_gather x2, waiting for transfers between devices, rows_first(): lax.all_gather(both, axis, axis=0, tiled=True)  51.9 us
    gather x2, local copies, waits for them, and re-layouts, local(): jnp.take(slot_values, bag.reshape(-1), axis=0).reshape(samples, -1)  15.8 us
    all_to_all x1, waiting for transfers between devices, local(): lax.all_to_all(packed, 'dev', split_axis=0, concat_axis=0, tiled=True)  13.7 us
    another operation x1, local copies, waits for them, and re-layouts, local(): jnp.stack([weight_one, weight_two])  13.4 us
    gather x2, local copies, waits for them, and re-layouts, local(): jnp.take(held_rows, next_bag.reshape(-1), axis=0)  12.2 us
    all_to_all x1, waiting for transfers between devices, local(): lax.all_to_all(returned, 'dev', split_axis=0, concat_axis=0, tiled=True)  9.17 us
  transfers between devices with their start and end apart: 6, of which 4 were waited for; matrix products, arithmetic and copies ran while one was open for 16% of the time, Pallas kernels for 0%

commit v1 on v0

v1 whole, which is shorter than its diff:
```python
import functools

import jax
import jax.numpy as jnp
from jax import lax
from jax.experimental import pallas as pl
from jax.experimental.pallas import tpu as pltpu
from jax.sharding import PartitionSpec as P

row_rate = 0.05
weight_rate = 0.005
bias_rate = 0.0002
epsilon = 1e-10

MESH = pl.DeviceIdType.MESH
F32 = jnp.float32
BF16 = jnp.bfloat16
HIGH = lax.Precision.HIGHEST
STRIDE = (32, 8, 2)
TILES = ((0, 1, 2, 6), (3, 4, 5, 7))
GATHER = ((0, 3, (2, 1, 0)), (3, 3, (1, 0, 2)), (6, 3, (0, 2, 1)))
GATHER_NEXT = ((0, 2, (2, 1, 0)), (2, 2, (1, 0, 2)), (4, 1, (0, 2, 1)))


def place():
    me = lax.axis_index("dev")
    core = lax.rem(me, 2)
    chip = me // 2
    coords = (chip // 16, lax.rem(chip // 4, 4), lax.rem(chip, 4))
    return me, core, coords


def step_to(me, coords, axis, by):
    at = coords[axis]
    return me + (lax.rem(at + by + 4, 4) - at) * STRIDE[axis]


def sibling_of(me, core):
    return me + 1 - 2 * core


def remote(source, target, send, recv, device):
    return pltpu.make_async_remote_copy(
        src_ref=source, dst_ref=target, send_sem=send, recv_sem=recv, device_id=(device,), device_id_type=MESH
    )


def greet(me, core, coords):
    barrier = pltpu.get_barrier_semaphore()
    for axis in range(3):
        for by in (1, -1):
            pl.semaphore_signal(barrier, inc=1, device_id=(step_to(me, coords, axis, by),), device_id_type=MESH)
    pl.semaphore_signal(barrier, inc=1, device_id=(sibling_of(me, core),), device_id_type=MESH)
    pl.semaphore_wait(barrier, 7)


def gather_all(buf, parts, me, core, coords, ring_send, ring_recv, pair_send, pair_recv):
    sends, pairs = [], []

    def view(part, index):
        first, count, _ = part
        return buf.at[(core, pl.ds(first, count), *index)]

    for k in range(3):
        firsts = []
        for p, part in enumerate(parts):
            axis, full = part[2][k], part[2][:k]

            def block(j, half=None, axis=axis, full=full):
                index = list(coords)
                for f in full:
                    index[f] = pl.ds(0, 4)
                if half is not None and full:
                    index[full[0]] = pl.ds(2 * half, 2)
                index[axis] = lax.rem(coords[axis] + j + 4, 4)
                return tuple(index)

            right, left = step_to(me, coords, axis, 1), step_to(me, coords, axis, -1)
            own = view(part, block(0))
            a = remote(own, own, ring_send.at[p, k, 0], ring_recv.at[p, k, 0], right)
            b = remote(own, own, ring_send.at[p, k, 1], ring_recv.at[p, k, 1], left)
            a.start()
            b.start()
            sends += [a, b]

            def pass_on(which, index, p=p, part=part):
                ref = view(part, index)
                copy = remote(ref, ref, pair_send.at[p, which], pair_recv.at[p, which], sibling_of(me, core))
                copy.start()
                pairs.append(copy)

            if k == 2:
                pass_on(0, block(0))
            firsts.append((p, part, a, b, block, right, left, pass_on))
        yield
        seconds = []
        for p, part, a, b, block, right, left, pass_on in firsts:
            a.wait_recv()
            ref = view(part, block(-1, 0))
            c = remote(ref, ref, ring_send.at[p, k, 2], ring_recv.at[p, k, 2], right)
            c.start()
            sends.append(c)
            b.wait_recv()
            d = None
            if k > 0:
                ref = view(part, block(1, 1))
                d = remote(ref, ref, ring_send.at[p, k, 3], ring_recv.at[p, k, 3], left)
                d.start()
                sends.append(d)
            if k == 2:
                pass_on(1, block(-1))
                pass_on(2, block(1))
            seconds.append((c, d, block, pass_on))
        yield
        for c, d, block, pass_on in seconds:
            c.wait_recv()
            if k == 2:
                pass_on(3, block(2, 0))
            if d is not None:
                d.wait_recv()
                if k == 2:
                    pass_on(4, block(2, 1))
    yield
    for copy in pairs:
        copy.wait_recv()
    for copy in sends + pairs:
        copy.wait_send()


def rows(value):
    return value.reshape(-1, value.shape[-1])


def front(
    w_ref, a_ref, b_ref, bag_ref, bag_t_ref, up_ref, hot_ref, evict_ref,
    wg_ref, hot_grad_ref, evict_grad_ref, pair_out,
    own, pair, buf, feat, feat_bf, proj, layer_bf, grad_two, grad_one, rest, grad_feat, values, bias_sum,
    ring_send, ring_recv, pair_send, pair_recv, swap_send, swap_recv,
):
    me, core, coords = place()
    for half in range(2):
        for layer in range(2):
            for j, t in enumerate(TILES[layer]):
                lanes = pl.ds(half * 512 + j * 128, 128)
                own[half, t] = w_ref[layer, :, lanes]
                own[half, 9 + t] = a_ref[layer, :, lanes]
        own[half, 8] = b_ref[...]
    greet(me, core, coords)
    mine = pl.ds(pl.multiple_of(core * 8, 8), 8)
    swap = remote(own.at[1 - core], pair.at[:, mine, :], swap_send, swap_recv, sibling_of(me, core))
    swap.start()
    pair[:, mine, :] = own[core]

    table = jnp.concatenate([hot_ref[...], evict_ref[...]], axis=0)
    high = table.astype(BF16)
    values[:, 0:128] = high
    values[:, 128:256] = (table - high.astype(F32)).astype(BF16)

    swap.wait_recv()
    buf[(core, slice(None), *coords)] = pair[0:9].astype(BF16)
    pair_out[...] = pair[...]

    def look_up(field):
        ids = bag_ref[:, field : field + 1]
        slots = lax.broadcasted_iota(jnp.int32, (ids.shape[0], 768), 1)
        pick = jnp.where(slots == ids, 1.0, 0.0).astype(BF16)
        found = jnp.dot(pick, values[...], preferred_element_type=F32)
        lanes = pl.ds(field * 128, 128)
        feat_bf[:, lanes] = found[:, 0:128].astype(BF16)
        value = found[:, 0:128] + found[:, 128:256]
        feat[:, lanes] = value
        two = up_ref[:, lanes].astype(F32) * value
        grad_two[:, lanes] = two.astype(BF16)
        bias_sum[1:2, lanes] = jnp.sum(two, axis=0, keepdims=True)

    bias_sum[...] = jnp.zeros_like(bias_sum)
    field = 0
    for _ in gather_all(buf, GATHER, me, core, coords, ring_send, ring_recv, pair_send, pair_recv):
        for _ in range(2):
            if field < 8:
                look_up(field)
                field += 1
    while field < 8:
        look_up(field)
        field += 1
    swap.wait_send()

    def by_rows(layer, block):
        return jnp.concatenate([rows(buf[h, t, block]) for h in range(2) for t in TILES[layer]], axis=1)

    def by_columns(layer, block):
        picked = TILES[layer][2 * (block % 2) : 2 * (block % 2) + 2]
        return jnp.concatenate([rows(buf[block // 2, t]) for t in picked], axis=1)

    def turned(a, b):
        return lax.dot_general(a, b, (((1,), (1,)), ((), ())), preferred_element_type=F32)

    def outer(a, b):
        return lax.dot_general(a, b, (((0,), (0,)), ((), ())), preferred_element_type=F32)

    def bias_of(layer, block):
        lane = lax.broadcasted_iota(jnp.int32, (8, 128), 1)
        pick = jnp.where(lane == layer, 1.0, 0.0).astype(BF16)
        return turned(pick, rows(buf[0, 8, block]))[0:1]

    def put(layer, block, value):
        value = value.astype(BF16)
        for h in range(2):
            for j, t in enumerate(TILES[layer]):
                at = h * 512 + j * 128
                wg_ref[h, t, block] = value[:, at : at + 128].reshape(4, 4, 16, 128)

    for n in range(4):
        lanes = pl.ds(n * 256, 256)
        one = turned(feat_bf[...], by_rows(0, n)) + bias_of(0, n)
        proj[:, lanes] = one
        value = feat[:, lanes]
        layer_bf[:, lanes] = (value * one + value).astype(BF16)
    for n in range(4):
        lanes = pl.ds(n * 256, 256)
        put(1, n, outer(grad_two[:, lanes], layer_bf[...]))
    for n in range(4):
        lanes = pl.ds(n * 256, 256)
        up = up_ref[:, lanes].astype(F32)
        back = up + jnp.dot(grad_two[...], by_columns(1, n), preferred_element_type=F32)
        one = back * feat[:, lanes]
        grad_one[:, lanes] = one.astype(BF16)
        bias_sum[0:1, lanes] = jnp.sum(one, axis=0, keepdims=True)
        two = turned(layer_bf[...], by_rows(1, n)) + bias_of(1, n)
        rest[:, lanes] = up * two + back * (proj[:, lanes] + 1.0)
    turned_sum = bias_sum[...].T.astype(BF16).reshape(4, 4, 4, 16, 128)
    wg_ref[0, 8] = turned_sum
    wg_ref[1, 8] = turned_sum
    for n in range(4):
        lanes = pl.ds(n * 256, 256)
        put(0, n, outer(grad_one[:, lanes], feat_bf[...]))
    for n in range(4):
        lanes = pl.ds(n * 256, 256)
        last = jnp.dot(grad_one[...], by_columns(0, n), preferred_element_type=F32)
        grad_feat[:, lanes] = (rest[:, lanes] + last).astype(BF16)
    total = jnp.zeros((768, 128), F32)
    for f in range(8):
        ids = bag_t_ref[f : f + 1, :]
        slots = lax.broadcasted_iota(jnp.int32, (768, ids.shape[1]), 0)
        pick = jnp.where(slots == ids, 1.0, 0.0).astype(BF16)
        total += jnp.dot(pick, grad_feat[:, f * 128 : f * 128 + 128], preferred_element_type=F32)
    hot_grad_ref[...] = total[0:512]
    evict_grad_ref[...] = total[512:768]


def middle(
    wg_ref, pair_ref, next_ref, w_new_ref, b_new_ref,
    sib, sums, got1, acc2, send2, got2, acc3, got3, total, buf, fresh, other,
    rs_send, rs_recv, sib_send, sib_recv, ring_send, ring_recv, pair_send, pair_recv, swap_send, swap_recv,
):
    me, core, coords = place()
    greet(me, core, coords)
    near = sibling_of(me, core)
    swaps, sends = [], []
    for p in range(3):
        tiles = pl.ds(3 * p, 3)
        copy = remote(wg_ref.at[1 - core, tiles], sib.at[tiles], sib_send.at[p], sib_recv.at[p], near)
        copy.start()
        swaps.append(copy)

    orders = [part[2][::-1] for part in GATHER]

    def launch(source, target, p, k, i, device):
        copy = remote(source, target, rs_send.at[p, k, i], rs_recv.at[p, k, i], device)
        copy.start()
        sends.append(copy)
        return copy

    def ends(p, k):
        axis = orders[p][k]
        return step_to(me, coords, axis, 1), step_to(me, coords, axis, -1)

    def pick(p, k, j, half=None):
        order = orders[p]
        axes = sorted(order[k:])
        index = []
        for axis in axes:
            if axis == order[k]:
                index.append(lax.rem(coords[axis] + j + 4, 4))
            elif half is not None and axis == order[2]:
                index.append(pl.ds(2 * half, 2))
            else:
                index.append(pl.ds(0, 4))
        return tuple(index)

    def inner(p, k, half):
        order = orders[p]
        axes = [axis for axis in sorted(order[k:]) if axis != order[k]]
        return tuple(pl.ds(2 * half, 2) if half is not None and axis == order[2] else pl.ds(0, 4) for axis in axes)

    def widen(value):
        return value.astype(F32)

    flights = []
    for p in range(3):
        tiles = pl.ds(3 * p, 3)
        swaps[p].wait_recv()
        for y in range(4):
            sums[tiles, y] = (widen(wg_ref[core, tiles, y]) + widen(sib[tiles, y])).astype(BF16)
        right, left = ends(p, 0)
        flights.append((
            launch(sums.at[(tiles, *pick(p, 0, 2, 0))], got1.at[(p, 0, slice(None), *inner(p, 0, 0))], p, 0, 0, right),
            launch(sums.at[(tiles, *pick(p, 0, 1, 1))], got1.at[(p, 1, slice(None), *inner(p, 0, 1))], p, 0, 1, right),
            launch(sums.at[(tiles, *pick(p, 0, 2, 1))], got1.at[(p, 0, slice(None), *inner(p, 0, 1))], p, 0, 2, left),
            launch(sums.at[(tiles, *pick(p, 0, -1, 0))], got1.at[(p, 2, slice(None), *inner(p, 0, 0))], p, 0, 3, left),
        ))
    later = []
    for p in range(3):
        tiles = pl.ds(3 * p, 3)
        right, left = ends(p, 0)
        first, _, third, _ = flights[p]
        pair_of = []
        for copy, j, half, slot, i, device in ((first, 1, 0, 1, 4, right), (third, -1, 1, 2, 5, left)):
            copy.wait_recv()
            at = (tiles, *pick(p, 0, j, half))
            there = (slice(None), *inner(p, 0, half))
            sums[at] = (widen(wg_ref[(core, *at)]) + widen(sib[at]) + widen(got1[(p, 0, *there)])).astype(BF16)
            pair_of.append(launch(sums.at[at], got1.at[(p, slot, *there)], p, 0, i, device))
        later.append(pair_of)
    for p in range(3):
        tiles = pl.ds(3 * p, 3)
        for copy in (flights[p][1], flights[p][3], *later[p]):
            copy.wait_recv()
        at = (tiles, *pick(p, 0, 0))
        acc2[p] = widen(wg_ref[(core, *at)]) + widen(sib[at]) + widen(got1[p, 1]) + widen(got1[p, 2])
        send2[p] = acc2[p].astype(BF16)
        right, left = ends(p, 1)
        flights[p] = (
            launch(send2.at[(p, slice(None), *pick(p, 1, 2, 0))], got2.at[(p, 0, slice(None), *inner(p, 1, 0))], p, 1, 0, right),
            launch(send2.at[(p, slice(None), *pick(p, 1, 1, 1))], got2.at[(p, 1, slice(None), *inner(p, 1, 1))], p, 1, 1, right),
            launch(send2.at[(p, slice(None), *pick(p, 1, 2, 1))], got2.at[(p, 0, slice(None), *inner(p, 1, 1))], p, 1, 2, left),
            launch(send2.at[(p, slice(None), *pick(p, 1, -1, 0))], got2.at[(p, 2, slice(None), *inner(p, 1, 0))], p, 1, 3, left),
        )
    for p in range(3):
        right, left = ends(p, 1)
        first, _, third, _ = flights[p]
        pair_of = []
        for copy, j, half, slot, i, device in ((first, 1, 0, 1, 4, right), (third, -1, 1, 2, 5, left)):
            copy.wait_recv()
            at = (p, slice(None), *pick(p, 1, j, half))
            there = (slice(None), *inner(p, 1, half))
            send2[at] = (acc2[at] + widen(got2[(p, 0, *there)])).astype(BF16)
            pair_of.append(launch(send2.at[at], got2.at[(p, slot, *there)], p, 1, i, device))
        later[p] = pair_of
    for p in range(3):
        for copy in (flights[p][1], flights[p][3], *later[p]):
            copy.wait_recv()
        acc3[p] = acc2[(p, slice(None), *pick(p, 1, 0))] + widen(got2[p, 1]) + widen(got2[p, 2])
        right, left = ends(p, 2)
        flights[p] = (
            launch(acc3.at[(p, slice(None), *pick(p, 2, 2))], got3.at[p, 0], p, 2, 0, right),
            launch(acc3.at[(p, slice(None), *pick(p, 2, -1))], got3.at[p, 2], p, 2, 3, left),
        )
    for p in range(3):
        right, left = ends(p, 2)
        flights[p][0].wait_recv()
        at = (p, slice(None), *pick(p, 2, 1))
        acc3[at] = acc3[at] + got3[p, 0]
        later[p] = launch(acc3.at[at], got3.at[p, 1], p, 2, 4, right)
    for p in range(3):
        flights[p][1].wait_recv()
        later[p].wait_recv()
        total[pl.ds(3 * p, 3)] = acc3[(p, slice(None), *pick(p, 2, 0))] + got3[p, 1] + got3[p, 2]

    grad = total[0:8]
    fresh[...] = pair_ref[0:8] - weight_rate * grad / (jnp.sqrt(pair_ref[9:17] + grad * grad) + epsilon)
    bias = pair_ref[8] - bias_rate * total[8]
    for j, t in enumerate(TILES[0]):
        buf[(core, j, *coords)] = fresh[t].astype(BF16)
    buf[(core, 4, *coords)] = bias.astype(BF16)
    mine = pl.ds(pl.multiple_of(core * 8, 8), 8)
    yours = pl.ds(pl.multiple_of(8 - core * 8, 8), 8)
    total[8] = bias
    b_new_ref[...] = total[8, mine, :]
    swap = remote(fresh.at[:, yours, :], other, swap_send, swap_recv, near)
    swap.start()
    for _ in gather_all(buf, GATHER_NEXT, me, core, coords, ring_send, ring_recv, pair_send, pair_recv):
        pass
    swap.wait()
    for layer in range(2):
        for h in range(2):
            for j, t in enumerate(TILES[layer]):
                at = h * 512 + j * 128
                w_new_ref[layer, :, at : at + 128] = jnp.where(core == h, fresh[t, mine, :], other[t])
    for h in range(2):
        for t in range(5):
            next_ref[h, t] = buf[h, t]
    for copy in swaps + sends:
        copy.wait_send()


def shared(ids_ref, arrived_ref, table_ref, accum_ref, new_ref, accum_new_ref, back_ref):
    wanted = lax.broadcasted_iota(jnp.int32, (512, 64), 1)
    pick = jnp.where(wanted == ids_ref[...], 1.0, 0.0)
    grad = lax.dot_general(pick, arrived_ref[...], (((0,), (0,)), ((), ())), precision=HIGH, preferred_element_type=F32)
    updated = accum_ref[...] + grad * grad
    new = table_ref[...] - row_rate * grad / (jnp.sqrt(updated) + epsilon)
    new_ref[...] = new
    accum_new_ref[...] = updated
    back_ref[...] = jnp.dot(pick, new, precision=HIGH, preferred_element_type=F32)


def owned(ids_ref, moved_ref, table_ref, accum_ref, new_ref, accum_new_ref):
    moved = moved_ref[...]
    for n in range(4):
        at = pl.ds(n * 256, 256)
        wanted = lax.broadcasted_iota(jnp.int32, (256, 256), 0) + n * 256
        pick = jnp.where(wanted == ids_ref[...], 1.0, 0.0)
        grad = jnp.dot(pick, moved, precision=HIGH, preferred_element_type=F32)
        updated = accum_ref[at, :] + grad * grad
        new_ref[at, :] = table_ref[at, :] - row_rate * grad / (jnp.sqrt(updated) + epsilon)
        accum_new_ref[at, :] = updated


def ahead(bag_ref, held_ref, next_ref, out_ref, values, feat, feat_bf):
    held = held_ref[...]
    high = held.astype(BF16)
    values[:, 0:128] = high
    values[:, 128:256] = (held - high.astype(F32)).astype(BF16)
    for f in range(8):
        ids = bag_ref[:, f : f + 1]
        slots = lax.broadcasted_iota(jnp.int32, (ids.shape[0], 512), 1)
        pick = jnp.where(slots == ids, 1.0, 0.0).astype(BF16)
        found = jnp.dot(pick, values[...], preferred_element_type=F32)
        lanes = pl.ds(f * 128, 128)
        feat_bf[:, lanes] = found[:, 0:128].astype(BF16)
        feat[:, lanes] = found[:, 0:128] + found[:, 128:256]
    nt = (((1,), (1,)), ((), ()))
    for n in range(4):
        lanes = pl.ds(n * 256, 256)
        weight = jnp.concatenate([rows(next_ref[h, t, n]) for h in range(2) for t in range(4)], axis=1)
        proj = lax.dot_general(feat_bf[...], weight, nt, preferred_element_type=F32)
        lane = lax.broadcasted_iota(jnp.int32, (8, 128), 1)
        pick = jnp.where(lane == 0, 1.0, 0.0).astype(BF16)
        proj = proj + lax.dot_general(pick, rows(next_ref[0, 4, n]), nt, preferred_element_type=F32)[0:1]
        value = feat[:, lanes]
        out_ref[:, lanes] = (value * proj + value).astype(BF16)


VM = pl.BlockSpec(memory_space=pltpu.VMEM)
DMA = pltpu.SemaphoreType.DMA
LIMIT = 60 * 1024 * 1024


def call(body, ins, outs, scratch, cost, collective=None):
    if collective is None:
        params = pltpu.CompilerParams(vmem_limit_bytes=LIMIT)
    else:
        params = pltpu.CompilerParams(vmem_limit_bytes=LIMIT, collective_id=collective, has_side_effects=True)
    return pl.pallas_call(
        body,
        out_shape=tuple(jax.ShapeDtypeStruct(s, d) for s, d in outs),
        in_specs=[VM] * ins,
        out_specs=tuple(VM for _ in outs),
        scratch_shapes=scratch,
        compiler_params=params,
        cost_estimate=pl.CostEstimate(flops=cost, bytes_accessed=8_000_000, transcendentals=0),
    )


def local(
    upstream, bag, next_bag, hot_slots, evict_dest, hot_cache, evict_cache, hot_table, hot_accum, owner_table, owner_accum,
    cross_w, cross_b, cross_accum,
):
    me = lax.axis_index("dev")
    biases = jnp.pad(cross_b.T, ((0, 0), (0, 126)))
    ids = hot_slots.reshape(128, 1, 4)
    arrived_ids = lax.all_to_all(ids, "dev", split_axis=0, concat_axis=0, tiled=True)
    local_ids = (arrived_ids - me * 64).reshape(512, 1)

    ring = [DMA((3, 3, 4)), DMA((3, 3, 4)), DMA((3, 5)), DMA((3, 5)), DMA, DMA]
    wide = (512, 1024)
    wg, hot_grad, evict_grad, pair = call(
        front, 8,
        [((2, 9, 4, 4, 4, 16, 128), BF16), ((512, 128), F32), ((256, 128), F32), ((17, 16, 128), F32)],
        [
            pltpu.VMEM((2, 17, 8, 128), F32), pltpu.VMEM((17, 16, 128), F32), pltpu.VMEM((2, 9, 4, 4, 4, 16, 128), BF16),
            pltpu.VMEM(wide, F32), pltpu.VMEM(wide, BF16), pltpu.VMEM(wide, F32), pltpu.VMEM(wide, BF16),
            pltpu.VMEM(wide, BF16), pltpu.VMEM(wide, BF16), pltpu.VMEM(wide, F32),
            pltpu.VMEM(wide, BF16), pltpu.VMEM((768, 256), BF16), pltpu.VMEM((128, 1024), F32), *ring,
        ],
        8_000_000_000, 1,
    )(
        jnp.swapaxes(cross_w, 1, 2), jnp.swapaxes(cross_accum, 1, 2), biases, bag, bag.T, upstream, hot_cache, evict_cache,
    )
    packed = jnp.concatenate([hot_grad.reshape(128, 4, 128), evict_grad.reshape(128, 2, 128)], axis=1)
    unpacked = lax.all_to_all(packed, "dev", split_axis=0, concat_axis=0, tiled=True)

    block = (4, 4, 16, 128)
    next_w, w_new, b_new = call(
        middle, 2,
        [((2, 5, 4, 4, 4, 16, 128), BF16), ((2, 8, 1024), F32), ((8, 128), F32)],
        [
            pltpu.VMEM((9, 4, 4, 4, 16, 128), BF16), pltpu.VMEM((9, 4, 4, 4, 16, 128), BF16),
            pltpu.VMEM((3, 3, 3, *block), BF16), pltpu.VMEM((3, 3, *block), F32), pltpu.VMEM((3, 3, *block), BF16),
            pltpu.VMEM((3, 3, 3, 4, 16, 128), BF16), pltpu.VMEM((3, 3, 4, 16, 128), F32),
            pltpu.VMEM((3, 3, 3, 16, 128), F32), pltpu.VMEM((9, 16, 128), F32),
            pltpu.VMEM((2, 5, 4, 4, 4, 16, 128), BF16), pltpu.VMEM((8, 16, 128), F32), pltpu.VMEM((8, 8, 128), F32),
            DMA((3, 3, 6)), DMA((3, 3, 6)), DMA((3,)), DMA((3,)), *ring,
        ],
        20_000_000_000, 2,
    )(wg, pair)

    hot_new, hot_accum_new, returned = call(
        shared, 4, [((64, 128), F32), ((64, 128), F32), ((512, 128), F32)], [], 100_000_000,
    )(local_ids, unpacked[:, :4].reshape(512, 128), hot_table, hot_accum)
    held = lax.all_to_all(returned.reshape(128, 4, 128), "dev", split_axis=0, concat_axis=0, tiled=True).reshape(512, 128)
    owner_new, owner_accum_new = call(
        owned, 4, [((1024, 128), F32), ((1024, 128), F32)], [], 1_000_000_000,
    )(evict_dest.reshape(1, 256), unpacked[:, 4:].reshape(256, 128), owner_table, owner_accum)
    (next_first,) = call(
        ahead, 3, [((512, 1024), BF16)],
        [pltpu.VMEM((512, 256), BF16), pltpu.VMEM(wide, F32), pltpu.VMEM(wide, BF16)], 3_000_000_000,
    )(next_bag, held, next_w)
    return (
        next_first, hot_new, hot_accum_new, owner_new, owner_accum_new,
        jnp.swapaxes(w_new, 1, 2), b_new[:, :2].T,
    )


def solution(mesh):
    row, cube = P("dev", None), P(None, None, "dev")
    return jax.shard_map(
        local,
        mesh=mesh,
        in_specs=(row, row, row, P("dev"), P("dev", None, None), row, row, row, row, row, row, cube, P(None, "dev"), cube),
        out_specs=(row, row, row, row, row, cube, P(None, "dev")),
        check_vma=False,
    )
```

time: 370 us -> 160 us (0.43)
  waiting for transfers between devices: 157 us -> 4.69 us
  Pallas kernels: 0 us -> 120 us
  blocking collectives: 68.7 us -> 0 us
  local copies, waits for them, and re-layouts: 64.8 us -> 10.9 us
  matrix products: 26 us -> 0 us
  other arithmetic: 21.8 us -> 2.1 us
  between operations: 14.3 us -> 0.72 us
  starting transfers between devices: 16.7 us -> 21.2 us
    pallas_call x0 -> x5, Pallas kernels: none -> 120 us  [the longest x1 62.3 us: local(): call(middle, 2, [((2, 5, 4, 4, 4, 16, 128), BF16), ((2, 8, 1024), F32), (...]
    unnamed x4 -> x0, waiting for transfers between devices: 82.3 us -> none
    unnamed x1 -> x0, blocking collectives: 68.7 us -> none
    all_gather x2 -> x0, waiting for transfers between devices: 51.9 us -> none  [rows_first(): lax.all_gather(both, axis, axis=0, tiled=True)]
    gather x5 -> x0, local copies, waits for them, and re-layouts: 29.1 us -> none  [the longest x2 15.8 us: local(): jnp.take(slot_values, bag.reshape(-1), axis=0).reshape(samples, -1)]
    dot_general x8 -> x0, matrix products: 26 us -> none  [the longest x1 5.3 us: local(): jnp.dot(next_feat.astype(jnp.bfloat16), first_weight, preferred_element_t...]
    all_to_all x1, waiting for transfers between devices: 13.7 us -> 0.01 us  [local(): lax.all_to_all(packed, 'dev', split_axis=0, concat_axis=0, tiled=True)]
    another operation x1 -> x0, local copies, waits for them, and re-layouts: 13.4 us -> none  [local(): jnp.stack([weight_one, weight_two])]
  transfers between devices with their start and end apart: 6 -> 3, of which waited for: 4 -> 1; matrix products, arithmetic and copies ran while one was open for 16% -> 6% of each run, Pallas kernels for 0% -> 70%
where the time goes in v1:
time: 160 us
  Pallas kernels  120 us (75%)
  starting transfers between devices  21.2 us (13%)
  local copies, waits for them, and re-layouts  10.9 us (7%)
  waiting for transfers between devices  4.69 us (3%)
  other arithmetic  2.1 us (1%)
    pallas_call x1, Pallas kernels, local(): call(middle, 2, [((2, 5, 4, 4, 4, 16, 128), BF16), ((2, 8, 1024), F32), (...  62.3 us
    pallas_call x1, Pallas kernels, local(): call(front, 8, [((2, 9, 4, 4, 4, 16, 128), BF16), ((512, 128), F32), ((25...  46.3 us
    all_to_all x1, starting transfers between devices, local(): lax.all_to_all(ids, 'dev', split_axis=0, concat_axis=0, tiled=True)  11.5 us
    pallas_call x1, Pallas kernels, local(): call(ahead, 3, [((512, 1024), BF16)], [pltpu.VMEM((512, 256), BF16), pltp...  5.64 us
    unnamed x14, local copies, waits for them, and re-layouts  5.24 us
    all_to_all x1, starting transfers between devices, local(): lax.all_to_all(returned.reshape(128, 4, 128), 'dev', split_axis=0, concat...  4.96 us
    all_to_all x1, starting transfers between devices, local(): lax.all_to_all(packed, 'dev', split_axis=0, concat_axis=0, tiled=True)  4.76 us
    all_to_all x1, waiting for transfers between devices, local(): lax.all_to_all(returned.reshape(128, 4, 128), 'dev', split_axis=0, concat...  4.68 us
  transfers between devices with their start and end apart: 3, of which 1 were waited for; matrix products, arithmetic and copies ran while one was open for 6% of the time, Pallas kernels for 70%

profile of v1, /device:TPU:1, one launch (start us, length us, event | category | flops | bytes accessed | tf_op | source)
XLA Modules:
  0.0 159.8 jit_solution(3457431579333637951)
XLA Ops:
  0.6 1.4 reshape.41
  2.0 11.5 %all-to-all-start = ((s32[128,1,4]{2,1,0:T(1,128)}), s32[128,1,4]{2,1,0:T(1,128)S(1)}, u32[]{:S(2)}, u32[]{:S(2)}) async-start(s32[128,1,4]{2,1,0:T(1,128)} %bitcast), calls=%async_computation | async-start | bytes 131072 | tf_op jit(solution)/shard_map/all_to_all | solution.py:473
  13.6 1.6 copy.34.bag_ref
  15.1 0.8 copy.33
  15.9 0.6 pad.4.b_ref
  16.5 46.3 %shard_map.189 = (bf16[2,9,4,4,4,16,128]{6,5,4,3,2,1,0:T(8,128)(2,1)}, f32[512,128]{1,0:T(8,128)}, f32[256,128]{1,0:T(8,128)}, f32[17,16,128]{2,1,0:T(8,128)}) custom-call(f32[2,8,1024]{2,1,0:T(8,128)} %bitcast.23, f32[2,8,1024]{2,1,0:T(8,128)} %bitcast.24, f32[8,128]{1,0:T(8,128)} %pad.4.b_ref, s32[512,8]{1,0:T(8,128)} %copy.34.bag_ref, s32[8,512]{1,0:T(8,128)} %bitcast.21, ...), custom_call_target="tpu_custom_call" | custom-call | flops 8000000000 | bytes 8000000 | tf_op jit(solution)/shard_map/pallas_call | solution.py:478
  62.8 1.9 %pad_maximum_fusion = f32[128,6,128]{2,1,0:T(8,128)} fusion(f32[128,2,128]{2,1,0:T(2,128)} %bitcast.18, f32[128,4,128]{2,1,0:T(4,128)} %bitcast.15), kind=kLoop, calls=%fused_computation | loop fusion | flops 98304 | bytes 786432 | tf_op jit(solution)/shard_map/concatenate | solution.py:491
  64.7 0.0 all-to-all-done
  64.7 4.8 %all-to-all-start.1 = ((f32[128,6,128]{2,1,0:T(8,128)}), f32[128,6,128]{2,1,0:T(8,128)S(1)}, u32[]{:S(2)}, u32[]{:S(2)}) async-start(f32[128,6,128]{2,1,0:T(8,128)} %pad_maximum_fusion), calls=%async_computation.1 | async-start | bytes 1048576 | tf_op jit(solution)/shard_map/all_to_all | solution.py:492
  69.5 0.0 copy-start.2
  69.5 0.0 copy-start.3
  69.5 62.3 %shard_map.191 = (bf16[2,5,4,4,4,16,128]{6,5,4,3,2,1,0:T(8,128)(2,1)}, f32[2,8,1024]{2,1,0:T(8,128)}, f32[8,128]{1,0:T(8,128)}) custom-call(bf16[2,9,4,4,4,16,128]{6,5,4,3,2,1,0:T(8,128)(2,1)} %get-tuple-element.22.wg_ref, f32[17,16,128]{2,1,0:T(8,128)} %get-tuple-element.23.pair_ref), custom_call_target="tpu_custom_call" | custom-call | flops 20000000000 | bytes 8000000 | tf_op jit(solution)/shard_map/pallas_call | solution.py:495
  131.8 0.0 copy-done.2
  131.8 0.8 copy.36.bag_ref
  132.6 0.2 subtract_reduce_fusion
  132.8 0.8 reshape.50.ids_ref
  133.6 0.0 all-to-all-done.1
  133.6 0.7 slice.12
  134.4 2.6 %shard_map.190 = (f32[64,128]{1,0:T(8,128)}, f32[64,128]{1,0:T(8,128)}, f32[512,128]{1,0:T(8,128)}) custom-call(s32[512,1]{1,0:T(8,128)} %reshape.50.ids_ref, f32[512,128]{1,0:T(8,128)} %bitcast.14, f32[64,128]{1,0:T(8,128)} %table_ref.2, f32[64,128]{1,0:T(8,128)} %accum_ref.2), custom_call_target="tpu_custom_call" | custom-call | flops 100000000 | bytes 8000000 | tf_op jit(solution)/shard_map/pallas_call | solution.py:509
  136.9 5.0 %all-to-all-start.2 = ((f32[128,4,128]{2,1,0:T(4,128)}), f32[128,4,128]{2,1,0:T(4,128)S(1)}, u32[]{:S(2)}, u32[]{:S(2)}) async-start(f32[128,4,128]{2,1,0:T(4,128)} %bitcast.17), calls=%async_computation.2 | async-start | bytes 524288 | tf_op jit(solution)/shard_map/all_to_all | solution.py:512
  141.9 0.7 slice_bitcast_fusion
  142.6 0.6 copy.38
  143.2 0.0 copy-done.3
  143.2 0.1 copy.37
  143.3 0.7 reshape.48.ids_ref
  144.0 0.7 slice.13
  144.8 3.4 %shard_map.193 = (f32[1024,128]{1,0:T(8,128)}, f32[1024,128]{1,0:T(8,128)}) custom-call(s32[1,256]{1,0:T(1,128)} %reshape.48.ids_ref, f32[256,128]{1,0:T(8,128)} %bitcast.19, f32[1024,128]{1,0:T(8,128)} %table_ref.3, f32[1024,128]{1,0:T(8,128)} %accum_ref.3), custom_call_target="tpu_custom_call" | custom-call | flops 1000000000 | bytes 8000000 | tf_op jit(solution)/shard_map/pallas_call | solution.py:513
  148.1 4.7 %all-to-all-done.2 = f32[128,4,128]{2,1,0:T(4,128)S(1)} async-done(((f32[128,4,128]{2,1,0:T(4,128)}), f32[128,4,128]{2,1,0:T(4,128)S(1)}, u32[]{:S(2)}, u32[]{:S(2)}) %all-to-all-start.2) | async-done | bytes 262176 | tf_op jit(solution)/shard_map/all_to_all | solution.py:512
  152.8 0.7 copy-done
  153.5 5.6 %shard_map.192 = bf16[512,1024]{1,0:T(8,128)(2,1)} custom-call(s32[512,8]{1,0:T(8,128)} %copy.36.bag_ref, f32[512,128]{1,0:T(8,128)} %bitcast.16, bf16[2,5,4,4,4,16,128]{6,5,4,3,2,1,0:T(8,128)(2,1)} %get-tuple-element.24.next_ref), custom_call_target="tpu_custom_call" | custom-call | flops 3000000000 | bytes 8000000 | tf_op jit(solution)/shard_map/pallas_call | solution.py:516
  159.2 0.0 copy-done.1
  159.2 0.6 copy.40
  (2 shorter events, 0.0 us)
Async XLA Ops:
  2.0 62.6 %all-to-all-start = ((s32[128,1,4]{2,1,0:T(1,128)}), s32[128,1,4]{2,1,0:T(1,128)S(1)}, u32[]{:S(2)}, u32[]{:S(2)}) async-start(s32[128,1,4]{2,1,0:T(1,128)} %bitcast), calls=%async_computation | async-start | bytes 131072 | tf_op jit(solution)/shard_map/all_to_all | solution.py:473
  64.7 68.9 %all-to-all-start.1 = ((f32[128,6,128]{2,1,0:T(8,128)}), f32[128,6,128]{2,1,0:T(8,128)S(1)}, u32[]{:S(2)}, u32[]{:S(2)}) async-start(f32[128,6,128]{2,1,0:T(8,128)} %pad_maximum_fusion), calls=%async_computation.1 | async-start | bytes 1048576 | tf_op jit(solution)/shard_map/all_to_all | solution.py:492
  69.5 62.3 %copy-start.2 = (s32[512,8]{0,1:T(8,128)S(1)}, s32[512,8]{0,1:T(8,128)}, u32[]{:S(2)}) copy-start(s32[512,8]{0,1:T(8,128)} %param.16) | copy-start | bytes 49156
  69.5 73.8 %copy-start.3 = (s32[1,128,2]{1,2,0:T(2,128)S(1)}, s32[1,128,2]{1,2,0:T(2,128)}, u32[]{:S(2)}) copy-start(s32[1,128,2]{1,2,0:T(2,128)} %param.18) | copy-start | bytes 3076
  136.9 15.9 %all-to-all-start.2 = ((f32[128,4,128]{2,1,0:T(4,128)}), f32[128,4,128]{2,1,0:T(4,128)S(1)}, u32[]{:S(2)}, u32[]{:S(2)}) async-start(f32[128,4,128]{2,1,0:T(4,128)} %bitcast.17), calls=%async_computation.2 | async-start | bytes 524288 | tf_op jit(solution)/shard_map/all_to_all | solution.py:512
  152.8 0.7 copy-start
  153.5 5.6 %copy-start.1 = (f32[2,8,1024]{2,1,0:T(8,128)S(1)}, f32[2,8,1024]{2,1,0:T(8,128)}, u32[]{:S(2)}) copy-start(f32[2,8,1024]{2,1,0:T(8,128)} %get-tuple-element.29) | copy-start | bytes 196612

commit v2 on v0

v2 whole, which is shorter than its diff:
```python
import jax
import jax.numpy as jnp
from jax import lax
from jax.experimental import pallas as pl
from jax.experimental.pallas import tpu as pltpu
from jax.sharding import PartitionSpec as P

row_rate = 0.05
weight_rate = 0.005
bias_rate = 0.0002
epsilon = 1e-10

MESH = pl.DeviceIdType.MESH
F32 = jnp.float32
BF16 = jnp.bfloat16
STRIDE = (32, 8, 2)
TILES = ((0, 1, 2, 6), (3, 4, 5, 7))
GATHER = ((0, 3, (2, 1, 0)), (3, 3, (1, 0, 2)), (6, 3, (0, 2, 1)))
GATHER_NEXT = ((0, 2, (2, 1, 0)), (2, 2, (1, 0, 2)), (4, 1, (0, 2, 1)))


def place():
    me = lax.axis_index("dev")
    core = lax.rem(me, 2)
    chip = me // 2
    coords = (chip // 16, lax.rem(chip // 4, 4), lax.rem(chip, 4))
    return me, core, coords


def step_to(me, coords, axis, by):
    at = coords[axis]
    return me + (lax.rem(at + by + 4, 4) - at) * STRIDE[axis]


def sibling_of(me, core):
    return me + 1 - 2 * core


def remote(source, target, send, recv, device):
    return pltpu.make_async_remote_copy(
        src_ref=source, dst_ref=target, send_sem=send, recv_sem=recv, device_id=(device,), device_id_type=MESH
    )


def greet(me, core):
    barrier = pltpu.get_barrier_semaphore()
    pl.semaphore_signal(barrier, inc=1, device_id=(sibling_of(me, core),), device_id_type=MESH)

    def one(i, carry):
        peer = lax.rem(me // 2 + i, 64)
        pl.semaphore_signal(barrier, inc=1, device_id=(peer * 2 + core,), device_id_type=MESH)
        return carry

    lax.fori_loop(1, 64, one, 0)


def all_here():
    pl.semaphore_wait(pltpu.get_barrier_semaphore(), 64)


LINES = (0, -1, 1, 2)
GOES_ON = (1, 1, -1, -1)


def gather_all(buf, parts, me, core, coords, ring_send, ring_recv, pair_send, pair_recv):
    sends, pairs, count = [], [], len(parts)
    near = sibling_of(me, core)

    def move(p, index, i, device):
        first, tiles, _ = parts[p]
        ref = buf.at[(core, pl.ds(first, tiles), *index)]
        copy = remote(ref, ref, ring_send.at[p, i], ring_recv.at[p, i], device)
        copy.start()
        sends.append(copy)
        return copy

    def pass_on(p, index, i):
        first, tiles, _ = parts[p]
        ref = buf.at[(core, pl.ds(first, tiles), *index)]
        copy = remote(ref, ref, pair_send.at[p, i], pair_recv.at[p, i], near)
        copy.start()
        pairs.append(copy)

    def index(p, **at):
        order = parts[p][2]
        out = list(coords)
        out[order[0]] = pl.ds(0, 4)
        if at.get("line") is None:
            out[order[1]] = pl.ds(0, 4)
        else:
            out[order[1]] = lax.rem(coords[order[1]] + at["line"] + 4, 4)
        out[order[2]] = lax.rem(coords[order[2]] + at.get("far", 0) + 4, 4)
        return tuple(out)

    def to(p, k, by):
        return step_to(me, coords, parts[p][2][k], by)

    one = [[move(p, coords, i, to(p, 0, by)) for i, by in enumerate((1, -1, 2))] for p in range(count)]
    yield
    two, right, left, passed = [], [], [], []

    def spread(p, i):
        where = index(p, line=LINES[i])
        right[p][i] = move(p, where, 6 + i, to(p, 2, 1))
        left[p][i] = move(p, where, 10 + i, to(p, 2, -1))

    for p in range(count):
        for copy in one[p]:
            copy.wait_recv()
        where = index(p, line=0)
        two.append([move(p, where, 3 + i, to(p, 1, by)) for i, by in enumerate((1, -1, 2))])
        right.append({})
        left.append({})
        passed.append({})
        spread(p, 0)
    yield

    def arrive(p, i):
        right[p][i].wait_recv()
        if GOES_ON[i] == 1:
            passed[p][i] = move(p, index(p, line=LINES[i], far=-1), 14 + i, to(p, 2, 1))
        pass_on(p, index(p, line=LINES[i], far=-1), 1 + i)
        left[p][i].wait_recv()
        if GOES_ON[i] == -1:
            passed[p][i] = move(p, index(p, line=LINES[i], far=1), 14 + i, to(p, 2, -1))
        pass_on(p, index(p, line=LINES[i], far=1), 5 + i)

    for i in (1, 2):
        for p in range(count):
            two[p][i - 1].wait_recv()
            spread(p, i)
    yield
    for p in range(count):
        arrive(p, 0)
    yield
    for p in range(count):
        two[p][2].wait_recv()
        spread(p, 3)
        pass_on(p, index(p), 0)
    yield
    for i in (1, 2, 3):
        for p in range(count):
            arrive(p, i)
        yield
    for i in range(4):
        for p in range(count):
            passed[p][i].wait_recv()
            pass_on(p, index(p, line=LINES[i], far=2), 9 + i)
        yield
    for copy in pairs:
        copy.wait_recv()
    for copy in sends + pairs:
        copy.wait_send()


def rows(value):
    return value.reshape(-1, value.shape[-1])


def turned(a, b):
    return lax.dot_general(a, b, (((1,), (1,)), ((), ())), preferred_element_type=F32)


def outer(a, b):
    return lax.dot_general(a, b, (((0,), (0,)), ((), ())), preferred_element_type=F32)


def iota(shape, dim):
    return lax.broadcasted_iota(jnp.int32, shape, dim)


def as_mask(hit, kind=BF16):
    return jnp.where(hit, 1.0, 0.0).astype(kind)


def halves_of(value):
    high = value.astype(BF16)
    return jnp.concatenate([high, (value - high.astype(F32)).astype(BF16)], axis=1)


def joined(value):
    return value[:, 0:128] + value[:, 128:256]


def widen(value):
    return value.astype(F32)


def step(
    w_ref, a_ref, b_ref, bag_t_ref, next_t_ref, ids_ref, dest_ref, up_ref, hot_ref, evict_ref, table_ref, accum_ref, owner_ref,
    owner_accum_ref,
    out_ref, hot_new_ref, hot_accum_new_ref, owner_new_ref, owner_accum_new_ref, w_new_ref, b_new_ref,
    own, pair, buf, bag, feat, feat_bf, proj, layer_bf, grad_two, grad_one, back, grad_feat, values, bias_sum,
    wg, sib, sums, got1, acc2, send2, got2, acc3, got3, total, fresh, other, buf_next,
    slots, arrived, gathered, split, reply, answer, held,
    ring_send, ring_recv, pair_send, pair_recv, swap_send, swap_recv,
    rs_send, rs_recv, sib_send, sib_recv, ring2_send, ring2_recv, pair2_send, pair2_recv,
    all_send, all_recv, near_send, near_recv,
):
    me, core, coords = place()
    chip = me // 2
    near = sibling_of(me, core)
    mine = pl.ds(pl.multiple_of(core * 8, 8), 8)
    yours = pl.ds(pl.multiple_of(8 - core * 8, 8), 8)

    greet(me, core)
    for half in range(2):
        for layer in range(2):
            for j, t in enumerate(TILES[layer]):
                lanes = pl.ds(half * 512 + j * 128, 128)
                own[half, t] = w_ref[layer, :, lanes]
                own[half, 9 + t] = a_ref[layer, :, lanes]
    bias_tile = jnp.zeros((8, 128), F32)
    for layer in range(2):
        spread = jnp.where(iota((8, 8), 0) == iota((8, 8), 1), jnp.broadcast_to(b_ref[layer : layer + 1, :], (8, 8)), 0.0)
        column = jnp.sum(spread, axis=1, keepdims=True)
        bias_tile = jnp.where(iota((8, 128), 1) == layer, column, bias_tile)
    own[0, 8] = bias_tile
    own[1, 8] = bias_tile
    values[0:512] = halves_of(hot_ref[...])
    values[512:768] = halves_of(evict_ref[...])
    bag[...] = bag_t_ref[...].T
    bias_sum[...] = jnp.zeros_like(bias_sum)
    all_here()
    swap = remote(own.at[1 - core], pair.at[:, mine, :], swap_send.at[0], swap_recv.at[0], near)
    swap.start()
    pair[:, mine, :] = own[core]
    swap.wait_recv()
    buf[(core, slice(None), *coords)] = pair[0:9].astype(BF16)

    def look_up(field):
        ids = bag[:, field : field + 1]
        found = jnp.dot(as_mask(iota((512, 768), 1) == ids), values[...], preferred_element_type=F32)
        lanes = pl.ds(field * 128, 128)
        feat_bf[:, lanes] = found[:, 0:128].astype(BF16)
        value = joined(found)
        feat[:, lanes] = value
        two = widen(up_ref[:, lanes]) * value
        grad_two[:, lanes] = two.astype(BF16)
        bias_sum[1:2, lanes] = jnp.sum(two, axis=0, keepdims=True)

    field = 0
    for _ in gather_all(buf, GATHER, me, core, coords, ring_send, ring_recv, pair_send, pair_recv):
        for _ in range(2):
            if field < 8:
                look_up(field)
                field += 1

    def by_rows(layer, block):
        return jnp.concatenate([rows(buf[h, t, block]) for h in range(2) for t in TILES[layer]], axis=1)

    def by_columns(layer, block):
        picked = TILES[layer][2 * (block % 2) : 2 * (block % 2) + 2]
        return jnp.concatenate([rows(buf[block // 2, t]) for t in picked], axis=1)

    def bias_of(layer, block):
        return turned(as_mask(iota((8, 128), 1) == layer), rows(buf[0, 8, block]))[0:1]

    def put(layer, block, value):
        value = value.astype(BF16)
        for h in range(2):
            for j, t in enumerate(TILES[layer]):
                at = h * 512 + j * 128
                wg[h, t, block] = value[:, at : at + 128].reshape(4, 4, 16, 128)

    orders = [part[2][::-1] for part in GATHER]
    sends, flights, later, thirds = [], {}, {}, {}

    def launch(source, target, p, i, device):
        copy = remote(source, target, rs_send.at[p, i], rs_recv.at[p, i], device)
        copy.start()
        sends.append(copy)
        return copy

    def to(p, k, by):
        return step_to(me, coords, orders[p][k], by)

    def pick(p, k, j, half=None):
        order, index = orders[p], []
        for axis in sorted(order[k:]):
            if axis == order[k]:
                index.append(lax.rem(coords[axis] + j + 4, 4))
            elif half is not None and axis == order[2]:
                index.append(pl.ds(2 * half, 2))
            else:
                index.append(pl.ds(0, 4))
        return tuple(index)

    def inner(p, half):
        order = orders[p]
        return tuple(pl.ds(2 * half, 2) if axis == order[2] else pl.ds(0, 4) for axis in sorted(order[1:]))

    def share(p):
        tiles = pl.ds(3 * p, 3)
        copy = remote(wg.at[1 - core, tiles], sib.at[tiles], sib_send.at[p], sib_recv.at[p], near)
        copy.start()
        sends.append(copy)
        flights[p] = copy

    def reduce_first(p):
        tiles = pl.ds(3 * p, 3)
        flights[p].wait_recv()
        for y in range(4):
            sums[tiles, y] = (widen(wg[core, tiles, y]) + widen(sib[tiles, y])).astype(BF16)

        def block(j, half, slot, i, by):
            at, there = (tiles, *pick(p, 0, j, half)), (slice(None), *inner(p, half))
            return launch(sums.at[at], got1.at[(p, slot, *there)], p, i, to(p, 0, by))

        flights[p] = (block(2, 0, 0, 0, 1), block(2, 1, 0, 2, -1), block(1, 1, 1, 1, 1), block(-1, 0, 2, 3, -1))

    def reduce_on(p):
        tiles = pl.ds(3 * p, 3)
        pair_of = []
        for copy, j, half, slot, i in ((flights[p][0], 1, 0, 1, 4), (flights[p][1], -1, 1, 2, 5)):
            copy.wait_recv()
            at, there = (tiles, *pick(p, 0, j, half)), (slice(None), *inner(p, half))
            sums[at] = (widen(wg[(core, *at)]) + widen(sib[at]) + widen(got1[(p, 0, *there)])).astype(BF16)
            pair_of.append(launch(sums.at[at], got1.at[(p, slot, *there)], p, i, to(p, 0, j)))
        later[p] = pair_of

    def reduce_second(p):
        for copy in (flights[p][2], flights[p][3], *later[p]):
            copy.wait_recv()
        at = (pl.ds(3 * p, 3), *pick(p, 0, 0))
        acc2[p] = widen(wg[(core, *at)]) + widen(sib[at]) + widen(got1[p, 1]) + widen(got1[p, 2])
        send2[p] = acc2[p].astype(BF16)
        flights[p] = [
            launch(send2.at[(p, slice(None), *pick(p, 1, by))], got2.at[p, i], p, 6 + i, to(p, 1, by))
            for i, by in enumerate((1, -1, 2))
        ]

    def reduce_third(p):
        for copy in flights[p]:
            copy.wait_recv()
        acc3[p] = acc2[(p, slice(None), *pick(p, 1, 0))] + widen(got2[p, 0]) + widen(got2[p, 1]) + widen(got2[p, 2])
        flights[p] = [
            launch(acc3.at[(p, slice(None), *pick(p, 2, by))], got3.at[p, i], p, 9 + i, to(p, 2, by))
            for i, by in enumerate((1, -1, 2))
        ]

    def reduce_last(p):
        for copy in flights[p]:
            copy.wait_recv()
        total[pl.ds(3 * p, 3)] = acc3[(p, slice(None), *pick(p, 2, 0))] + got3[p, 0] + got3[p, 1] + got3[p, 2]

    for n in range(4):
        lanes = pl.ds(n * 256, 256)
        value = widen(up_ref[:, lanes]) + jnp.dot(grad_two[...], by_columns(1, n), preferred_element_type=F32)
        back[:, lanes] = value
        one = value * feat[:, lanes]
        grad_one[:, lanes] = one.astype(BF16)
        bias_sum[0:1, lanes] = jnp.sum(one, axis=0, keepdims=True)
    turned_sum = bias_sum[...].T.astype(BF16).reshape(4, 4, 4, 16, 128)
    wg[0, 8] = turned_sum
    wg[1, 8] = turned_sum
    for n in range(4):
        put(0, n, outer(grad_one[:, n * 256 : n * 256 + 256], feat_bf[...]))
    share(0)
    for n in range(4):
        lanes = pl.ds(n * 256, 256)
        one = turned(feat_bf[...], by_rows(0, n)) + bias_of(0, n)
        proj[:, lanes] = one
        value = feat[:, lanes]
        layer_bf[:, lanes] = (value * one + value).astype(BF16)
    reduce_first(0)
    for n in range(4):
        put(1, n, outer(grad_two[:, n * 256 : n * 256 + 256], layer_bf[...]))
    share(1)
    share(2)
    reduce_on(0)

    def second(n):
        lanes = pl.ds(n * 256, 256)
        two = turned(layer_bf[...], by_rows(1, n)) + bias_of(1, n)
        back[:, lanes] = widen(up_ref[:, lanes]) * two + back[:, lanes] * (proj[:, lanes] + 1.0)

    def last(n):
        lanes = pl.ds(n * 256, 256)
        rest = jnp.dot(grad_one[...], by_columns(0, n), preferred_element_type=F32)
        grad_feat[:, lanes] = (back[:, lanes] + rest).astype(BF16)

    second(0)
    second(1)
    second(2)
    reduce_first(1)
    reduce_first(2)
    second(3)
    reduce_second(0)
    last(0)
    last(1)
    last(2)
    last(3)
    reduce_on(1)
    reduce_on(2)

    owner, k = iota((1024, 128), 0) >> 3, iota((1024, 128), 0) & 7
    key = jnp.where(k < 4, owner * 4 + k, jnp.where(k < 6, 512 + owner * 2 + k - 4, -1))
    key = jnp.concatenate([key] * 4, axis=1)
    summed = jnp.zeros((1024, 128), F32)
    for f in range(8):
        ids = bag_t_ref[f : f + 1, :]
        summed += jnp.dot(as_mask(key == ids), grad_feat[:, f * 128 : f * 128 + 128], preferred_element_type=F32)
        if f == 3:
            reduce_third(0)
    slots[...] = summed.reshape(64, 2, 8, 128)
    place_of = as_mask((iota((128, 128), 0) & 3) == iota((128, 128), 1))
    for a in range(4):
        number = (ids_ref[a : a + 1, :] - (a * 32 + (iota((1, 128), 1) >> 2)) * 64).astype(F32)
        row, lane = iota((256, 128), 0), iota((256, 128), 1)
        keep = ((row & 7) == 6) & ((lane >> 2) == (row >> 3))
        numbers = jnp.dot(jnp.where(keep, number, 0.0).astype(BF16), place_of, preferred_element_type=F32)
        part = pl.ds(a * 16, 16)
        slots[part] = slots[part] + numbers.reshape(16, 2, 8, 128)

    def to_chips(source, target, sem):
        def one(i, carry):
            peer = lax.rem(chip + i, 64)
            remote(source.at[peer], target.at[chip], all_send.at[sem], all_recv.at[sem], peer * 2 + core).start()
            return carry

        lax.fori_loop(1, 64, one, 0)
        target[chip] = source[chip]
        many = pl.ds(0, 63)
        return remote(source.at[many], target.at[many], all_send.at[sem], all_recv.at[sem], near)

    outward = to_chips(slots, arrived, 0)
    reduce_second(1)
    reduce_second(2)
    reduce_last(0)
    reduce_third(1)
    reduce_third(2)
    reduce_last(1)
    reduce_last(2)

    grad = total[0:8]
    fresh[...] = pair[0:8] - weight_rate * grad / (jnp.sqrt(pair[9:17] + grad * grad) + epsilon)
    bias = pair[8] - bias_rate * total[8]
    for j, t in enumerate(TILES[0]):
        buf_next[(core, j, *coords)] = fresh[t].astype(BF16)
    buf_next[(core, 4, *coords)] = bias.astype(BF16)
    following = gather_all(buf_next, GATHER_NEXT, me, core, coords, ring2_send, ring2_recv, pair2_send, pair2_recv)
    next(following)
    swap_new = remote(fresh.at[:, yours, :], other, swap_send.at[1], swap_recv.at[1], near)
    swap_new.start()
    total[8] = bias
    new_bias = total[8, mine, :]
    for layer in range(2):
        column = jnp.broadcast_to(new_bias[:, layer : layer + 1], (8, 8))
        turned_bias = jnp.where(iota((8, 8), 0) == iota((8, 8), 1), column, 0.0)
        b_new_ref[layer : layer + 1, :] = jnp.sum(turned_bias, axis=0, keepdims=True)

    outward.wait_recv()
    cross = remote(arrived.at[:, 1 - core], gathered.at[:, core], near_send.at[0], near_recv.at[0], near)
    cross.start()
    gathered[:, core] = arrived[:, core]
    next(following)
    cross.wait_recv()
    split[...] = halves_of(gathered[...].reshape(1024, 128))
    numbers = jnp.broadcast_to(gathered[:, :, 6:7, :].reshape(128, 1, 128), (128, 8, 128)).reshape(1024, 128)
    wanted = jnp.where((iota((1024, 128), 0) & 3) == iota((1024, 128), 1), numbers, 0.0)
    number = jnp.sum(wanted, axis=1, keepdims=True).astype(jnp.int32)
    lane, k = iota((1024, 128), 1), iota((1024, 128), 0) & 7
    hit = as_mask(lane == number + jnp.where(k < 4, 0, 64))
    hot_grad = joined(outer(hit, split[...]))[0:64]
    updated = accum_ref[...] + hot_grad * hot_grad
    hot_new = table_ref[...] - row_rate * hot_grad / (jnp.sqrt(updated) + epsilon)
    hot_new_ref[...] = hot_new
    hot_accum_new_ref[...] = updated
    high = hot_new.astype(BF16)
    both = jnp.concatenate([high, (hot_new - high.astype(F32)).astype(BF16)], axis=0)
    reply[...] = jnp.dot(hit, both, preferred_element_type=F32).astype(BF16).reshape(64, 2, 8, 128)
    return_near = remote(reply.at[:, 1 - core], answer.at[:, core], near_send.at[1], near_recv.at[1], near)
    return_near.start()
    answer[:, core] = reply[:, core]
    next(following)
    return_near.wait_recv()
    homeward = to_chips(answer, held, 1)
    next(following)

    bound = jnp.concatenate([dest_ref[0:1, :], dest_ref[1:2, :]], axis=1) + 1
    came_at = (iota((256, 1024), 0) & 127) * 8 + 4 + (iota((256, 1024), 0) >> 7)
    lay = as_mask(came_at == iota((256, 1024), 1))

    def laid(number):
        number = jnp.broadcast_to(number.astype(F32), (8, 256)).astype(BF16)
        return jnp.dot(number, lay, preferred_element_type=F32)[0:1]

    target = (laid(bound >> 5) * 32.0 + laid(bound & 31)).astype(jnp.int32)
    for n in range(4):
        at = pl.ds(n * 256, 256)
        hit = as_mask(iota((256, 1024), 0) + (n * 256 + 1) == target)
        owner_grad = joined(jnp.dot(hit, split[...], preferred_element_type=F32))
        updated = owner_accum_ref[at, :] + owner_grad * owner_grad
        owner_new_ref[at, :] = owner_ref[at, :] - row_rate * owner_grad / (jnp.sqrt(updated) + epsilon)
        owner_accum_new_ref[at, :] = updated
        next(following)
    bag[...] = next_t_ref[...].T

    homeward.wait_recv()
    key = (iota((1, 1024), 1) >> 3) * 4 + (iota((1, 1024), 1) & 3)
    for f in range(8):
        hit = as_mask(bag[:, f : f + 1] == key)
        value = jnp.dot(hit, held[...].reshape(1024, 128), preferred_element_type=F32)
        lanes = pl.ds(f * 128, 128)
        feat[:, lanes] = value
        feat_bf[:, lanes] = value.astype(BF16)
        if f % 2:
            next(following, None)
    for _ in following:
        pass
    for n in range(4):
        lanes = pl.ds(n * 256, 256)
        weight = jnp.concatenate([rows(buf_next[h, t, n]) for h in range(2) for t in range(4)], axis=1)
        bias = turned(as_mask(iota((8, 128), 1) == 0), rows(buf_next[0, 4, n]))[0:1]
        value = feat[:, lanes]
        out_ref[:, lanes] = (value * (turned(feat_bf[...], weight) + bias) + value).astype(BF16)
    swap_new.wait_recv()
    for layer in range(2):
        for h in range(2):
            for j, t in enumerate(TILES[layer]):
                at = h * 512 + j * 128
                w_new_ref[layer, :, at : at + 128] = jnp.where(core == h, fresh[t, mine, :], other[t])
    for copy in (swap, swap_new, cross, return_near, outward, homeward, *sends):
        copy.wait_send()


VM = pl.BlockSpec(memory_space=pltpu.VMEM)
DMA = pltpu.SemaphoreType.DMA


def local(
    upstream, bag, next_bag, hot_slots, evict_dest, hot_cache, evict_cache, hot_table, hot_accum, owner_table, owner_accum,
    cross_w, cross_b, cross_accum,
):
    wide, cube, block = (512, 1024), (9, 4, 4, 4, 16, 128), (4, 4, 16, 128)
    ring = [DMA((3, 18)), DMA((3, 18)), DMA((3, 13)), DMA((3, 13))]
    unit = (64, 2, 8, 128)
    outs = [
        (wide, BF16), ((64, 128), F32), ((64, 128), F32), ((1024, 128), F32), ((1024, 128), F32), ((2, 8, 1024), F32), ((2, 8), F32),
    ]
    scratch = [
        ((2, 17, 8, 128), F32), ((17, 16, 128), F32), ((2, *cube), BF16), ((512, 8), jnp.int32), (wide, F32), (wide, BF16),
        (wide, F32), (wide, BF16), (wide, BF16), (wide, BF16), (wide, F32), (wide, BF16), ((768, 256), BF16), ((128, 1024), F32),
        ((2, *cube), BF16), (cube, BF16), (cube, BF16), ((3, 3, 3, *block), BF16), ((3, 3, *block), F32), ((3, 3, *block), BF16),
        ((3, 3, 3, 4, 16, 128), BF16), ((3, 3, 4, 16, 128), F32), ((3, 3, 3, 16, 128), F32), ((9, 16, 128), F32),
        ((8, 16, 128), F32), ((8, 8, 128), F32), ((2, 5, *cube[1:]), BF16),
        (unit, F32), (unit, F32), (unit, F32), ((1024, 256), BF16), (unit, BF16), (unit, BF16), (unit, BF16),
    ]
    results = pl.pallas_call(
        step,
        out_shape=tuple(jax.ShapeDtypeStruct(s, d) for s, d in outs),
        in_specs=[VM] * 14,
        out_specs=tuple(VM for _ in outs),
        scratch_shapes=[
            *(pltpu.VMEM(s, d) for s, d in scratch),
            *ring, DMA((2,)), DMA((2,)), DMA((3, 12)), DMA((3, 12)), DMA((3,)), DMA((3,)), *ring,
            DMA((2,)), DMA((2,)), DMA((2,)), DMA((2,)),
        ],
        compiler_params=pltpu.CompilerParams(vmem_limit_bytes=60 * 1024 * 1024, collective_id=1, has_side_effects=True),
        cost_estimate=pl.CostEstimate(flops=12_000_000_000, bytes_accessed=12_000_000, transcendentals=0),
    )(
        jnp.swapaxes(cross_w, 1, 2), jnp.swapaxes(cross_accum, 1, 2), cross_b, bag.T, next_bag.T, hot_slots.reshape(4, 128),
        evict_dest[0].T, upstream, hot_cache, evict_cache, hot_table, hot_accum, owner_table, owner_accum,
    )
    return (*results[:5], jnp.swapaxes(results[5], 1, 2), results[6])


def solution(mesh):
    row, cube = P("dev", None), P(None, None, "dev")
    return jax.shard_map(
        local,
        mesh=mesh,
        in_specs=(row, row, row, P("dev"), P("dev", None, None), row, row, row, row, row, row, cube, P(None, "dev"), cube),
        out_specs=(row, row, row, row, row, cube, P(None, "dev")),
        check_vma=False,
    )
```

time: 370 us -> 102 us (0.28)
  waiting for transfers between devices: 157 us -> 0 us
  Pallas kernels: 0 us -> 93.8 us
  blocking collectives: 68.7 us -> 0 us
  local copies, waits for them, and re-layouts: 64.8 us -> 7 us
  matrix products: 26 us -> 0 us
  other arithmetic: 21.8 us -> 0 us
  starting transfers between devices: 16.7 us -> 0 us
  between operations: 14.3 us -> 0.67 us
    pallas_call x0 -> x1, Pallas kernels: none -> 93.8 us  [local(): pl.pallas_call(step, out_shape=tuple((jax.ShapeDtypeStruct(s, d) for s, d...]
    unnamed x4 -> x0, waiting for transfers between devices: 82.3 us -> none
    unnamed x1 -> x0, blocking collectives: 68.7 us -> none
    all_gather x2 -> x0, waiting for transfers between devices: 51.9 us -> none  [rows_first(): lax.all_gather(both, axis, axis=0, tiled=True)]
    gather x5 -> x0, local copies, waits for them, and re-layouts: 29.1 us -> none  [the longest x2 15.8 us: local(): jnp.take(slot_values, bag.reshape(-1), axis=0).reshape(samples, -1)]
    dot_general x8 -> x0, matrix products: 26 us -> none  [the longest x1 5.3 us: local(): jnp.dot(next_feat.astype(jnp.bfloat16), first_weight, preferred_element_t...]
    all_to_all x3 -> x0, waiting for transfers between devices: 22.8 us -> none  [the longest x1 13.7 us: local(): lax.all_to_all(packed, 'dev', split_axis=0, concat_axis=0, tiled=True)]
    all_to_all x3 -> x0, starting transfers between devices: 16.6 us -> none  [the longest x1 6.63 us: local(): lax.all_to_all(packed, 'dev', split_axis=0, concat_axis=0, tiled=True)]
  transfers between devices with their start and end apart: 6 -> 0, of which waited for: 4 -> 0; matrix products, arithmetic and copies ran while one was open for 16% -> 0% of each run, Pallas kernels for 0% -> 0%
where the time goes in v2:
time: 102 us; the launch traced here: 101 us
  Pallas kernels  93.8 us (92%)
  local copies, waits for them, and re-layouts  7 us (7%)
    pallas_call x1, Pallas kernels, local(): pl.pallas_call(step, out_shape=tuple((jax.ShapeDtypeStruct(s, d) for s, d...  93.8 us
    unnamed x19, local copies, waits for them, and re-layouts  7 us

profile of v2, /device:TPU:1, one launch (start us, length us, event | category | flops | bytes accessed | tf_op | source)
XLA Modules:
  0.0 101.4 jit_solution(489046083649517559)
XLA Ops:
  0.6 93.8 %shard_map.189 = (bf16[512,1024]{1,0:T(8,128)(2,1)}, f32[64,128]{1,0:T(8,128)}, f32[64,128]{1,0:T(8,128)}, f32[1024,128]{1,0:T(8,128)}, f32[1024,128]{1,0:T(8,12...) custom-call(f32[2,8,1024]{2,1,0:T(8,128)} %bitcast.10, f32[2,8,1024]{2,1,0:T(8,128)} %bitcast.11, f32[2,8]{1,0:T(2,128)} %b_ref.1, ...), custom_call_target="tpu_custom_call" | custom-call | flops 12000000000 | bytes 12000000 | tf_op jit(solution)/shard_map/pallas_call | solution.py:550
  94.4 0.0 copy-start.4
  94.4 0.0 copy-start.1
  94.4 2.3 %copy.28 = bf16[512,1024]{1,0:T(8,128)(2,1)} copy(bf16[512,1024]{1,0:T(8,128)(2,1)} %get-tuple-element.28) | data formatting | bytes 2097152
  96.7 0.0 copy-done.4
  96.7 0.0 copy-start.3
  96.7 0.6 copy.29
  97.4 0.2 copy-done.3
  97.5 0.6 copy.30
  98.1 0.0 copy-done.1
  98.1 0.0 copy-start
  98.1 0.8 copy.31
  98.9 0.4 copy-done
  99.4 0.0 copy-start.2
  99.4 0.8 copy.32
  100.2 0.1 copy-done.2
  100.2 0.0 copy-start.5
  100.2 0.6 copy.33
  100.9 0.0 copy-done.5
  100.9 0.6 copy.34
Async XLA Ops:
  94.4 2.3 %copy-start.4 = (f32[64,128]{1,0:T(8,128)S(1)}, f32[64,128]{1,0:T(8,128)}, u32[]{:S(2)}) copy-start(f32[64,128]{1,0:T(8,128)} %get-tuple-element.29) | copy-start | bytes 98308
  94.4 3.7 %copy-start.1 = (f32[1024,128]{1,0:T(8,128)S(1)}, f32[1024,128]{1,0:T(8,128)}, u32[]{:S(2)}) copy-start(f32[1024,128]{1,0:T(8,128)} %get-tuple-element.31) | copy-start | bytes 1572868
  96.7 0.8 copy-start.3
  98.1 1.2 %copy-start = (f32[1024,128]{1,0:T(8,128)S(1)}, f32[1024,128]{1,0:T(8,128)}, u32[]{:S(2)}) copy-start(f32[1024,128]{1,0:T(8,128)} %get-tuple-element.32) | copy-start | bytes 1572868
  99.4 0.9 copy-start.2
  100.2 0.6 copy-start.5

commit v3 on v2

--- a/solution.py
+++ b/solution.py
@@ -14,8 +14,10 @@
 F32 = jnp.float32
 BF16 = jnp.bfloat16
 STRIDE = (32, 8, 2)
-TILES = ((0, 1, 2, 6), (3, 4, 5, 7))
+TILES = ((0, 1, 2, 3), (5, 6, 7, 8))
+BIAS = 4
 GATHER = ((0, 3, (2, 1, 0)), (3, 3, (1, 0, 2)), (6, 3, (0, 2, 1)))
+REDUCE = ((0, 2, (0, 1, 2)), (2, 2, (2, 0, 1)), (4, 1, (1, 2, 0)), (5, 1, (0, 1, 2)), (6, 1, (2, 0, 1)), (7, 2, (1, 2, 0)))
 GATHER_NEXT = ((0, 2, (2, 1, 0)), (2, 2, (1, 0, 2)), (4, 1, (0, 2, 1)))
 
 
@@ -42,20 +44,16 @@
     )
 
 
-def greet(me, core):
+def greet(me, core, coords):
     barrier = pltpu.get_barrier_semaphore()
     pl.semaphore_signal(barrier, inc=1, device_id=(sibling_of(me, core),), device_id_type=MESH)
-
-    def one(i, carry):
-        peer = lax.rem(me // 2 + i, 64)
-        pl.semaphore_signal(barrier, inc=1, device_id=(peer * 2 + core,), device_id_type=MESH)
-        return carry
-
-    lax.fori_loop(1, 64, one, 0)
+    for axis in range(3):
+        for by in (1, -1, 2):
+            pl.semaphore_signal(barrier, inc=1, device_id=(step_to(me, coords, axis, by),), device_id_type=MESH)
 
 
 def all_here():
-    pl.semaphore_wait(pltpu.get_barrier_semaphore(), 64)
+    pl.semaphore_wait(pltpu.get_barrier_semaphore(), 10)
 
 
 LINES = (0, -1, 1, 2)
@@ -203,20 +201,20 @@
     mine = pl.ds(pl.multiple_of(core * 8, 8), 8)
     yours = pl.ds(pl.multiple_of(8 - core * 8, 8), 8)
 
-    greet(me, core)
+    greet(me, core, coords)
     for half in range(2):
         for layer in range(2):
             for j, t in enumerate(TILES[layer]):
                 lanes = pl.ds(half * 512 + j * 128, 128)
                 own[half, t] = w_ref[layer, :, lanes]
-                own[half, 9 + t] = a_ref[layer, :, lanes]
+                own[half, 9 + 4 * layer + j] = a_ref[layer, :, lanes]
     bias_tile = jnp.zeros((8, 128), F32)
     for layer in range(2):
         spread = jnp.where(iota((8, 8), 0) == iota((8, 8), 1), jnp.broadcast_to(b_ref[layer : layer + 1, :], (8, 8)), 0.0)
         column = jnp.sum(spread, axis=1, keepdims=True)
         bias_tile = jnp.where(iota((8, 128), 1) == layer, column, bias_tile)
-    own[0, 8] = bias_tile
-    own[1, 8] = bias_tile
+    own[0, BIAS] = bias_tile
+    own[1, BIAS] = bias_tile
     values[0:512] = halves_of(hot_ref[...])
     values[512:768] = halves_of(evict_ref[...])
     bag[...] = bag_t_ref[...].T
@@ -254,7 +252,7 @@
         return jnp.concatenate([rows(buf[block // 2, t]) for t in picked], axis=1)
 
     def bias_of(layer, block):
-        return turned(as_mask(iota((8, 128), 1) == layer), rows(buf[0, 8, block]))[0:1]
+        return turned(as_mask(iota((8, 128), 1) == layer), rows(buf[0, BIAS, block]))[0:1]
 
     def put(layer, block, value):
         value = value.astype(BF16)
@@ -263,8 +261,9 @@
                 at = h * 512 + j * 128
                 wg[h, t, block] = value[:, at : at + 128].reshape(4, 4, 16, 128)
 
-    orders = [part[2][::-1] for part in GATHER]
-    sends, flights, later, thirds = [], {}, {}, {}
+    orders = [part[2] for part in REDUCE]
+    spans = [pl.ds(part[0], part[1]) for part in REDUCE]
+    sends, flights, later = [], {}, {}
 
     def launch(source, target, p, i, device):
         copy = remote(source, target, rs_send.at[p, i], rs_recv.at[p, i], device)
@@ -291,58 +290,60 @@
         return tuple(pl.ds(2 * half, 2) if axis == order[2] else pl.ds(0, 4) for axis in sorted(order[1:]))
 
     def share(p):
-        tiles = pl.ds(3 * p, 3)
-        copy = remote(wg.at[1 - core, tiles], sib.at[tiles], sib_send.at[p], sib_recv.at[p], near)
+        copy = remote(wg.at[1 - core, spans[p]], sib.at[spans[p]], sib_send.at[p], sib_recv.at[p], near)
         copy.start()
         sends.append(copy)
         flights[p] = copy
 
     def reduce_first(p):
-        tiles = pl.ds(3 * p, 3)
         flights[p].wait_recv()
-        for y in range(4):
-            sums[tiles, y] = (widen(wg[core, tiles, y]) + widen(sib[tiles, y])).astype(BF16)
 
         def block(j, half, slot, i, by):
-            at, there = (tiles, *pick(p, 0, j, half)), (slice(None), *inner(p, half))
-            return launch(sums.at[at], got1.at[(p, slot, *there)], p, i, to(p, 0, by))
+            at, there = (spans[p], *pick(p, 0, j, half)), (slot, spans[p], *inner(p, half))
+            sums[at] = (widen(wg[(core, *at)]) + widen(sib[at])).astype(BF16)
+            return launch(sums.at[at], got1.at[there], p, i, to(p, 0, by))
 
         flights[p] = (block(2, 0, 0, 0, 1), block(2, 1, 0, 2, -1), block(1, 1, 1, 1, 1), block(-1, 0, 2, 3, -1))
 
     def reduce_on(p):
-        tiles = pl.ds(3 * p, 3)
         pair_of = []
         for copy, j, half, slot, i in ((flights[p][0], 1, 0, 1, 4), (flights[p][1], -1, 1, 2, 5)):
             copy.wait_recv()
-            at, there = (tiles, *pick(p, 0, j, half)), (slice(None), *inner(p, half))
-            sums[at] = (widen(wg[(core, *at)]) + widen(sib[at]) + widen(got1[(p, 0, *there)])).astype(BF16)
-            pair_of.append(launch(sums.at[at], got1.at[(p, slot, *there)], p, i, to(p, 0, j)))
+            at, there = (spans[p], *pick(p, 0, j, half)), (spans[p], *inner(p, half))
+            sums[at] = (widen(wg[(core, *at)]) + widen(sib[at]) + widen(got1[(0, *there)])).astype(BF16)
+            pair_of.append(launch(sums.at[at], got1.at[(slot, *there)], p, i, to(p, 0, j)))
         later[p] = pair_of
 
     def reduce_second(p):
         for copy in (flights[p][2], flights[p][3], *later[p]):
             copy.wait_recv()
-        at = (pl.ds(3 * p, 3), *pick(p, 0, 0))
-        acc2[p] = widen(wg[(core, *at)]) + widen(sib[at]) + widen(got1[p, 1]) + widen(got1[p, 2])
-        send2[p] = acc2[p].astype(BF16)
+        span, at = spans[p], (spans[p], *pick(p, 0, 0))
+        acc2[span] = widen(wg[(core, *at)]) + widen(sib[at]) + widen(got1[1, span]) + widen(got1[2, span])
+        send2[span] = acc2[span].astype(BF16)
         flights[p] = [
-            launch(send2.at[(p, slice(None), *pick(p, 1, by))], got2.at[p, i], p, 6 + i, to(p, 1, by))
-            for i, by in enumerate((1, -1, 2))
+            launch(send2.at[(span, *pick(p, 1, by))], got2.at[i, span], p, 6 + i, to(p, 1, by)) for i, by in enumerate((1, -1, 2))
         ]
 
     def reduce_third(p):
         for copy in flights[p]:
             copy.wait_recv()
-        acc3[p] = acc2[(p, slice(None), *pick(p, 1, 0))] + widen(got2[p, 0]) + widen(got2[p, 1]) + widen(got2[p, 2])
+        span = spans[p]
+        acc3[span] = acc2[(span, *pick(p, 1, 0))] + widen(got2[0, span]) + widen(got2[1, span]) + widen(got2[2, span])
         flights[p] = [
-            launch(acc3.at[(p, slice(None), *pick(p, 2, by))], got3.at[p, i], p, 9 + i, to(p, 2, by))
-            for i, by in enumerate((1, -1, 2))
+            launch(acc3.at[(span, *pick(p, 2, by))], got3.at[i, span], p, 9 + i, to(p, 2, by)) for i, by in enumerate((1, -1, 2))
         ]
 
     def reduce_last(p):
         for copy in flights[p]:
             copy.wait_recv()
-        total[pl.ds(3 * p, 3)] = acc3[(p, slice(None), *pick(p, 2, 0))] + got3[p, 0] + got3[p, 1] + got3[p, 2]
+        span = spans[p]
+        total[span] = acc3[(span, *pick(p, 2, 0))] + got3[0, span] + got3[1, span] + got3[2, span]
+
+    def every(stage, parts):
+        for p in parts:
+            stage(p)
+
+    early, late = (0, 1, 2), (3, 4, 5)
 
     for n in range(4):
         lanes = pl.ds(n * 256, 256)
@@ -352,23 +353,21 @@
         grad_one[:, lanes] = one.astype(BF16)
         bias_sum[0:1, lanes] = jnp.sum(one, axis=0, keepdims=True)
     turned_sum = bias_sum[...].T.astype(BF16).reshape(4, 4, 4, 16, 128)
-    wg[0, 8] = turned_sum
-    wg[1, 8] = turned_sum
+    wg[0, BIAS] = turned_sum
+    wg[1, BIAS] = turned_sum
     for n in range(4):
         put(0, n, outer(grad_one[:, n * 256 : n * 256 + 256], feat_bf[...]))
-    share(0)
+    every(share, early)
     for n in range(4):
         lanes = pl.ds(n * 256, 256)
         one = turned(feat_bf[...], by_rows(0, n)) + bias_of(0, n)
         proj[:, lanes] = one
         value = feat[:, lanes]
         layer_bf[:, lanes] = (value * one + value).astype(BF16)
-    reduce_first(0)
     for n in range(4):
         put(1, n, outer(grad_two[:, n * 256 : n * 256 + 256], layer_bf[...]))
-    share(1)
-    share(2)
-    reduce_on(0)
+    every(share, late)
+    every(reduce_first, early)
 
     def second(n):
         lanes = pl.ds(n * 256, 256)
@@ -380,19 +379,13 @@
         rest = jnp.dot(grad_one[...], by_columns(0, n), preferred_element_type=F32)
         grad_feat[:, lanes] = (back[:, lanes] + rest).astype(BF16)
 
-    second(0)
-    second(1)
-    second(2)
-    reduce_first(1)
-    reduce_first(2)
-    second(3)
-    reduce_second(0)
+    for n in range(4):
+        second(n)
     last(0)
     last(1)
+    every(reduce_on, early)
     last(2)
     last(3)
-    reduce_on(1)
-    reduce_on(2)
 
     owner, k = iota((1024, 128), 0) >> 3, iota((1024, 128), 0) & 7
     key = jnp.where(k < 4, owner * 4 + k, jnp.where(k < 6, 512 + owner * 2 + k - 4, -1))
@@ -402,7 +395,8 @@
         ids = bag_t_ref[f : f + 1, :]
         summed += jnp.dot(as_mask(key == ids), grad_feat[:, f * 128 : f * 128 + 128], preferred_element_type=F32)
         if f == 3:
-            reduce_third(0)
+            every(reduce_first, late)
+    every(reduce_second, early)
     slots[...] = summed.reshape(64, 2, 8, 128)
     place_of = as_mask((iota((128, 128), 0) & 3) == iota((128, 128), 1))
     for a in range(4):
@@ -425,26 +419,25 @@
         return remote(source.at[many], target.at[many], all_send.at[sem], all_recv.at[sem], near)
 
     outward = to_chips(slots, arrived, 0)
-    reduce_second(1)
-    reduce_second(2)
-    reduce_last(0)
-    reduce_third(1)
-    reduce_third(2)
-    reduce_last(1)
-    reduce_last(2)
-
-    grad = total[0:8]
-    fresh[...] = pair[0:8] - weight_rate * grad / (jnp.sqrt(pair[9:17] + grad * grad) + epsilon)
-    bias = pair[8] - bias_rate * total[8]
-    for j, t in enumerate(TILES[0]):
-        buf_next[(core, j, *coords)] = fresh[t].astype(BF16)
-    buf_next[(core, 4, *coords)] = bias.astype(BF16)
+    every(reduce_on, late)
+    every(reduce_third, early)
+    every(reduce_second, late)
+    every(reduce_last, early)
+
+    def renew(layer):
+        tiles = pl.ds(TILES[layer][0], 4)
+        grad, squares = total[tiles], pair[9 + 4 * layer : 13 + 4 * layer]
+        fresh[tiles] = pair[tiles] - weight_rate * grad / (jnp.sqrt(squares + grad * grad) + epsilon)
+        copy = remote(fresh.at[tiles, yours, :], other.at[tiles], swap_send.at[1 + layer], swap_recv.at[1 + layer], near)
+        copy.start()
+        return copy
+
+    renewed = renew(0)
+    fresh[BIAS] = pair[BIAS] - bias_rate * total[BIAS]
+    buf_next[(core, slice(None), *coords)] = fresh[0:5].astype(BF16)
     following = gather_all(buf_next, GATHER_NEXT, me, core, coords, ring2_send, ring2_recv, pair2_send, pair2_recv)
     next(following)
-    swap_new = remote(fresh.at[:, yours, :], other, swap_send.at[1], swap_recv.at[1], near)
-    swap_new.start()
-    total[8] = bias
-    new_bias = total[8, mine, :]
+    new_bias = fresh[BIAS, mine, :]
     for layer in range(2):
         column = jnp.broadcast_to(new_bias[:, layer : layer + 1], (8, 8))
         turned_bias = jnp.where(iota((8, 8), 0) == iota((8, 8), 1), column, 0.0)
@@ -477,6 +470,7 @@
     return_near.wait_recv()
     homeward = to_chips(answer, held, 1)
     next(following)
+    every(reduce_third, late)
 
     bound = jnp.concatenate([dest_ref[0:1, :], dest_ref[1:2, :]], axis=1) + 1
     came_at = (iota((256, 1024), 0) & 127) * 8 + 4 + (iota((256, 1024), 0) >> 7)
@@ -495,6 +489,8 @@
         owner_new_ref[at, :] = owner_ref[at, :] - row_rate * owner_grad / (jnp.sqrt(updated) + epsilon)
         owner_accum_new_ref[at, :] = updated
         next(following)
+    every(reduce_last, late)
+    renewed_too = renew(1)
     bag[...] = next_t_ref[...].T
 
     homeward.wait_recv()
@@ -515,17 +511,33 @@
         bias = turned(as_mask(iota((8, 128), 1) == 0), rows(buf_next[0, 4, n]))[0:1]
         value = feat[:, lanes]
         out_ref[:, lanes] = (value * (turned(feat_bf[...], weight) + bias) + value).astype(BF16)
-    swap_new.wait_recv()
+    renewed.wait_recv()
+    renewed_too.wait_recv()
     for layer in range(2):
         for h in range(2):
             for j, t in enumerate(TILES[layer]):
                 at = h * 512 + j * 128
                 w_new_ref[layer, :, at : at + 128] = jnp.where(core == h, fresh[t, mine, :], other[t])
-    for copy in (swap, swap_new, cross, return_near, outward, homeward, *sends):
+    for copy in (swap, renewed, renewed_too, cross, return_near, outward, homeward, *sends):
         copy.wait_send()
 
 
+def keep(*refs):
+    count = (len(refs) - 2) // 3
+    came, gone = refs[-2:]
+    loads = [pltpu.make_async_copy(refs[i], refs[2 * count + i], came.at[i]) for i in range(count)]
+    stores = [pltpu.make_async_copy(refs[2 * count + i], refs[count + i], gone.at[i]) for i in range(count)]
+    for copy in loads:
+        copy.start()
+    for load, store in zip(loads, stores):
+        load.wait()
+        store.start()
+    for copy in stores:
+        copy.wait()
+
+
 VM = pl.BlockSpec(memory_space=pltpu.VMEM)
+ANY = pl.BlockSpec(memory_space=pl.ANY)
 DMA = pltpu.SemaphoreType.DMA
 
 
@@ -542,9 +554,9 @@
     scratch = [
         ((2, 17, 8, 128), F32), ((17, 16, 128), F32), ((2, *cube), BF16), ((512, 8), jnp.int32), (wide, F32), (wide, BF16),
         (wide, F32), (wide, BF16), (wide, BF16), (wide, BF16), (wide, F32), (wide, BF16), ((768, 256), BF16), ((128, 1024), F32),
-        ((2, *cube), BF16), (cube, BF16), (cube, BF16), ((3, 3, 3, *block), BF16), ((3, 3, *block), F32), ((3, 3, *block), BF16),
-        ((3, 3, 3, 4, 16, 128), BF16), ((3, 3, 4, 16, 128), F32), ((3, 3, 3, 16, 128), F32), ((9, 16, 128), F32),
-        ((8, 16, 128), F32), ((8, 8, 128), F32), ((2, 5, *cube[1:]), BF16),
+        ((2, *cube), BF16), (cube, BF16), (cube, BF16), ((3, 9, *block), BF16), ((9, *block), F32), ((9, *block), BF16),
+        ((3, 9, 4, 16, 128), BF16), ((9, 4, 16, 128), F32), ((3, 9, 16, 128), F32), ((9, 16, 128), F32),
+        ((9, 16, 128), F32), ((9, 8, 128), F32), ((2, 5, *cube[1:]), BF16),
         (unit, F32), (unit, F32), (unit, F32), ((1024, 256), BF16), (unit, BF16), (unit, BF16), (unit, BF16),
     ]
     results = pl.pallas_call(
@@ -554,7 +566,7 @@
         out_specs=tuple(VM for _ in outs),
         scratch_shapes=[
             *(pltpu.VMEM(s, d) for s, d in scratch),
-            *ring, DMA((2,)), DMA((2,)), DMA((3, 12)), DMA((3, 12)), DMA((3,)), DMA((3,)), *ring,
+            *ring, DMA((3,)), DMA((3,)), DMA((6, 12)), DMA((6, 12)), DMA((6,)), DMA((6,)), *ring,
             DMA((2,)), DMA((2,)), DMA((2,)), DMA((2,)),
         ],
         compiler_params=pltpu.CompilerParams(vmem_limit_bytes=60 * 1024 * 1024, collective_id=1, has_side_effects=True),
@@ -563,6 +575,13 @@
         jnp.swapaxes(cross_w, 1, 2), jnp.swapaxes(cross_accum, 1, 2), cross_b, bag.T, next_bag.T, hot_slots.reshape(4, 128),
         evict_dest[0].T, upstream, hot_cache, evict_cache, hot_table, hot_accum, owner_table, owner_accum,
     )
+    results = pl.pallas_call(
+        keep,
+        out_shape=tuple(jax.ShapeDtypeStruct(s, d) for s, d in outs),
+        in_specs=[ANY] * len(outs),
+        out_specs=tuple(ANY for _ in outs),
+        scratch_shapes=[*(pltpu.VMEM(s, d) for s, d in outs), DMA((len(outs),)), DMA((len(outs),))],
+    )(*results)
     return (*results[:5], jnp.swapaxes(results[5], 1, 2), results[6])
 
 

time: 102 us -> 89.5 us (0.88)
  local copies, waits for them, and re-layouts: 7 us -> 0 us
  Pallas kernels: 93.8 us -> 88.5 us
    pallas_call x1, Pallas kernels: 93.8 us -> 85.8 us  [local(): pl.pallas_call(step, out_shape=tuple((jax.ShapeDtypeStruct(s, d) for s, d...]
    unnamed x19 -> x0, local copies, waits for them, and re-layouts: 7 us -> none
    pallas_call x0 -> x1, Pallas kernels: none -> 2.69 us  [local(): pl.pallas_call(keep, out_shape=tuple((jax.ShapeDtypeStruct(s, d) for s, d...]
where the time goes in v3:
time: 89.5 us; the launch traced here: 89.3 us
  Pallas kernels  88.5 us (99%)
    pallas_call x1, Pallas kernels, local(): pl.pallas_call(step, out_shape=tuple((jax.ShapeDtypeStruct(s, d) for s, d...  85.8 us
    pallas_call x1, Pallas kernels, local(): pl.pallas_call(keep, out_shape=tuple((jax.ShapeDtypeStruct(s, d) for s, d...  2.69 us

profile of v3, /device:TPU:1, one launch (start us, length us, event | category | flops | bytes accessed | tf_op | source)
XLA Modules:
  0.0 89.3 jit_solution(9843748586616449677)
XLA Ops:
  0.6 85.8 %shard_map.189 = (bf16[512,1024]{1,0:T(8,128)(2,1)}, f32[64,128]{1,0:T(8,128)}, f32[64,128]{1,0:T(8,128)}, f32[1024,128]{1,0:T(8,128)}, f32[1024,128]{1,0:T(8,12...) custom-call(f32[2,8,1024]{2,1,0:T(8,128)} %bitcast.9, f32[2,8,1024]{2,1,0:T(8,128)} %bitcast.10, f32[2,8]{1,0:T(2,128)} %b_ref.1, ...), custom_call_target="tpu_custom_call" | custom-call | flops 12000000000 | bytes 12000000 | tf_op jit(solution)/shard_map/pallas_call | solution.py:562
  86.5 2.7 %shard_map.190 = (bf16[512,1024]{1,0:T(8,128)(2,1)}, f32[64,128]{1,0:T(8,128)}, f32[64,128]{1,0:T(8,128)}, f32[1024,128]{1,0:T(8,128)}, f32[1024,128]{1,0:T(8,12...) custom-call(bf16[512,1024]{1,0:T(8,128)(2,1)} %get-tuple-element.21.refs_0_, f32[64,128]{1,0:T(8,128)} %get-tuple-element.22.refs_1_, ...), custom_call_target="tpu_custom_call" | custom-call | tf_op jit(solution)/shard_map/pallas_call | solution.py:578

commit v4 on v3

--- a/solution.py
+++ b/solution.py
@@ -238,8 +238,8 @@
         bias_sum[1:2, lanes] = jnp.sum(two, axis=0, keepdims=True)
 
     field = 0
-    for _ in gather_all(buf, GATHER, me, core, coords, ring_send, ring_recv, pair_send, pair_recv):
-        for _ in range(2):
+    for turn, _ in enumerate(gather_all(buf, GATHER, me, core, coords, ring_send, ring_recv, pair_send, pair_recv)):
+        for _ in range((3, 3, 1, 1)[min(turn, 3)]):
             if field < 8:
                 look_up(field)
                 field += 1
@@ -489,8 +489,6 @@
         owner_new_ref[at, :] = owner_ref[at, :] - row_rate * owner_grad / (jnp.sqrt(updated) + epsilon)
         owner_accum_new_ref[at, :] = updated
         next(following)
-    every(reduce_last, late)
-    renewed_too = renew(1)
     bag[...] = next_t_ref[...].T
 
     homeward.wait_recv()
@@ -505,6 +503,8 @@
             next(following, None)
     for _ in following:
         pass
+    every(reduce_last, late)
+    renewed_too = renew(1)
     for n in range(4):
         lanes = pl.ds(n * 256, 256)
         weight = jnp.concatenate([rows(buf_next[h, t, n]) for h in range(2) for t in range(4)], axis=1)

time: 89.5 us -> 89 us (level)
  no operation moved by 1% of the time
where the time goes in v4:
time: 89 us; the launch traced here: 88.8 us
  Pallas kernels  88 us (99%)
    pallas_call x1, Pallas kernels, local(): pl.pallas_call(step, out_shape=tuple((jax.ShapeDtypeStruct(s, d) for s, d...  85.3 us
    pallas_call x1, Pallas kernels, local(): pl.pallas_call(keep, out_shape=tuple((jax.ShapeDtypeStruct(s, d) for s, d...  2.69 us

profile of v4, /device:TPU:1, one launch (start us, length us, event | category | flops | bytes accessed | tf_op | source)
XLA Modules:
  0.0 88.8 jit_solution(7261140717107297303)
XLA Ops:
  0.6 85.3 %shard_map.189 = (bf16[512,1024]{1,0:T(8,128)(2,1)}, f32[64,128]{1,0:T(8,128)}, f32[64,128]{1,0:T(8,128)}, f32[1024,128]{1,0:T(8,128)}, f32[1024,128]{1,0:T(8,12...) custom-call(f32[2,8,1024]{2,1,0:T(8,128)} %bitcast.9, f32[2,8,1024]{2,1,0:T(8,128)} %bitcast.10, f32[2,8]{1,0:T(2,128)} %b_ref.1, ...), custom_call_target="tpu_custom_call" | custom-call | flops 12000000000 | bytes 12000000 | tf_op jit(solution)/shard_map/pallas_call | solution.py:562
  86.0 2.7 %shard_map.190 = (bf16[512,1024]{1,0:T(8,128)(2,1)}, f32[64,128]{1,0:T(8,128)}, f32[64,128]{1,0:T(8,128)}, f32[1024,128]{1,0:T(8,128)}, f32[1024,128]{1,0:T(8,12...) custom-call(bf16[512,1024]{1,0:T(8,128)(2,1)} %get-tuple-element.21.refs_0_, f32[64,128]{1,0:T(8,128)} %get-tuple-element.22.refs_1_, ...), custom_call_target="tpu_custom_call" | custom-call | tf_op jit(solution)/shard_map/pallas_call | solution.py:578
